TPU v7x, 256 devices: a whole 4x4x8 slice. The times are simulated.
256 devices in a mesh: seq: 8 (over y, core), dp: 32 (over z, x).
Axes of the slice: x: 4, y: 4, z: 8, core: 2. Of those that a mesh axis runs over, the one named last changes fastest.
Arguments:
- q_rows: bfloat16 [32768, 2048], P(('seq', 'dp')), may hold values from -6 to 6
- key_rows: bfloat16 [32768, 512], P(('seq', 'dp')), may hold values from -6 to 6
- value_rows: bfloat16 [32768, 512], P(('seq', 'dp')), may hold values from -6 to 6
- pack_peer: int32 [4096], P(('seq', 'dp')), may hold values from 0 to 31, as said below
- pack_slot: int32 [4096], P(('seq', 'dp')), may hold values from 0 to 15
- doc_ids: int32 [32, 1024], P('dp'), may hold values from 0 to 7, never falling along the last dimension, each value on 1 to 512 neighbouring positions
- grad_out: bfloat16 [32, 1024, 2048], P('dp', 'seq'), may hold values from -6 to 6
- out_weight: bfloat16 [2048, 2048], P(('seq', 'dp')), may hold values from -0.125 to 0.125
Outputs:
- dq_rows: bfloat16 [32768, 2048], P(('seq', 'dp'))
- key_gradient_rows: bfloat16 [32768, 512], P(('seq', 'dp'))
- value_gradient_rows: bfloat16 [32768, 512], P(('seq', 'dp'))
- wo_grad: float32 [2048, 2048], P(('seq', 'dp'))
Inputs may be any that keep to these rules, and one draw needn't show every extreme that they name: `pack_peer`: blocks keep their seq index; every block position of every packed sequence receives exactly one block; the 16 blocks of one device send at most 1 block to one packed sequence, and exactly 1 to some.
All inputs are finite; a program needn't handle non-finite values.
Results may differ from a plain program's by a relative error of at most 0.03.
Values may be sent and summed in bfloat16 or wider, within the bound.
A program may use at most 64 MiB of HBM per device.

v0:
```python
import math

import jax
import jax.numpy as jnp
from jax import lax
from jax.sharding import PartitionSpec as P

HEAD_SIZE = 128
PACK = 8
QBLK = 512


NEG_FILL = -1e30


def body(q_rows, key_rows, value_rows, pack_peer, pack_slot, doc_ids, grad_out, out_weight):
    seq_count = lax.axis_size("seq")
    dp_count = lax.axis_size("dp")
    tok_dev = q_rows.shape[0]
    kv_heads = key_rows.shape[1] // HEAD_SIZE
    block_count = pack_peer.shape[0]
    capacity = (block_count + dp_count - 1) // dp_count
    soft_scale = 1.0 / math.sqrt(HEAD_SIZE)
    grad_scale = 8.0 / math.sqrt(dp_count * seq_count * tok_dev)
    same_peer = pack_peer[:, None] == pack_peer[None, :]
    earlier = lax.broadcasted_iota(jnp.int32, (block_count, block_count), 1) < lax.broadcasted_iota(
        jnp.int32, (block_count, block_count), 0
    )
    peer_rank = jnp.sum((same_peer & earlier).astype(jnp.int32), axis=1)
    send_index = pack_peer * capacity + peer_rank

    def to_slots(sample_rows):
        columns = sample_rows.shape[1]
        head_grouped = sample_rows.reshape(block_count, PACK, columns)
        blank = jnp.zeros((dp_count * capacity, PACK, columns), sample_rows.dtype)
        return blank.at[send_index].set(head_grouped)

    slot_tag = (
        jnp.full((dp_count * capacity,), block_count, jnp.int32).at[send_index].set(pack_slot)
    )
    slot_tag = slot_tag.astype(jnp.bfloat16).reshape(dp_count, capacity)
    came_q, came_k, came_v, came_tag = (
        lax.all_to_all(to_slots(q_rows), "dp", split_axis=0, concat_axis=0, tiled=True),
        lax.all_to_all(to_slots(key_rows), "dp", split_axis=0, concat_axis=0, tiled=True),
        lax.all_to_all(to_slots(value_rows), "dp", split_axis=0, concat_axis=0, tiled=True),
        lax.all_to_all(slot_tag, "dp", split_axis=0, concat_axis=0, tiled=True),
    )
    landing = came_tag.reshape(-1).astype(jnp.int32)

    def from_slots(arrived):
        columns = arrived.shape[2]
        blank = jnp.zeros((block_count, PACK, columns), arrived.dtype)
        return blank.at[landing].set(arrived, mode="drop").reshape(tok_dev, columns)

    packed_q = from_slots(came_q)
    packed_keys = from_slots(came_k)
    packed_values = from_slots(came_v)
    repeat_count = seq_count // kv_heads

    def widen(packed_rows):
        split_heads = packed_rows.reshape(tok_dev, kv_heads, HEAD_SIZE)
        return jnp.repeat(split_heads, repeat_count, axis=1).reshape(tok_dev, seq_count * HEAD_SIZE)

    head_q, head_k, head_v = (
        lax.all_to_all(packed_q, "seq", split_axis=1, concat_axis=0, tiled=True),
        lax.all_to_all(widen(packed_keys), "seq", split_axis=1, concat_axis=0, tiled=True),
        lax.all_to_all(widen(packed_values), "seq", split_axis=1, concat_axis=0, tiled=True),
    )
    seq_len = head_q.shape[0]
    head_group = head_q.shape[1] // HEAD_SIZE
    query_blocks = seq_len // QBLK
    doc_full = doc_ids[0]
    firsts = doc_full.reshape(query_blocks, QBLK)[:, 0]
    key_starts = jnp.sum((doc_full[None, :] < firsts[:, None]).astype(jnp.int32), axis=1) // QBLK
    q_blocks = head_q.reshape(query_blocks, QBLK, head_group, HEAD_SIZE)
    local_pos = lax.broadcasted_iota(jnp.int32, (QBLK,), 0)

    def block_scores(q_block, q_index, k_index):
        k_block = lax.dynamic_slice_in_dim(head_k, k_index * QBLK, QBLK, 0)
        raw = (
            jnp.einsum("qgd,kd->gqk", q_block, k_block, preferred_element_type=jnp.float32)
            * soft_scale
        )
        q_docs = lax.dynamic_slice_in_dim(doc_full, q_index * QBLK, QBLK, 0)
        k_docs = lax.dynamic_slice_in_dim(doc_full, k_index * QBLK, QBLK, 0)
        q_pos = q_index * QBLK + local_pos
        k_pos = k_index * QBLK + local_pos
        allowed = (q_docs[:, None] == k_docs[None, :]) & (q_pos[:, None] >= k_pos[None, :])
        return (jnp.where(allowed[None], raw, NEG_FILL), allowed, k_block)

    def lse_block(q_index):
        q_block = q_blocks[q_index]

        def lse_advance(k_index, state):
            running_top, running_total = state
            masked, allowed, k_block = block_scores(q_block, q_index, k_index)
            new_top = jnp.maximum(running_top, jnp.max(masked, axis=2))
            terms = jnp.where(allowed[None], jnp.exp(masked - new_top[:, :, None]), 0.0)
            running_total = running_total * jnp.exp(running_top - new_top) + jnp.sum(terms, axis=2)
            return (new_top, running_total)

        start_state = (
            jnp.full((head_group, QBLK), NEG_FILL, jnp.float32),
            jnp.zeros((head_group, QBLK), jnp.float32),
        )
        final_top, final_total = lax.fori_loop(
            key_starts[q_index], q_index + 1, lse_advance, start_state
        )
        return final_top + jnp.log(final_total)

    block_ids = jnp.arange(query_blocks, dtype=jnp.int32)
    log_totals = lax.map(lse_block, block_ids)

    def output_block(q_index):
        q_block = q_blocks[q_index]
        row_lse = log_totals[q_index]

        def output_advance(k_index, summed):
            masked, allowed, k_block = block_scores(q_block, q_index, k_index)
            v_block = lax.dynamic_slice_in_dim(head_v, k_index * QBLK, QBLK, 0)
            weights_low = jnp.where(
                allowed[None], jnp.exp(masked - row_lse[:, :, None]), 0.0
            ).astype(jnp.bfloat16)
            return summed + jnp.einsum(
                "gqk,kd->gqd", weights_low, v_block, preferred_element_type=jnp.float32
            )

        summed = lax.fori_loop(
            key_starts[q_index],
            q_index + 1,
            output_advance,
            jnp.zeros((head_group, QBLK, HEAD_SIZE), jnp.float32),
        )
        return jnp.transpose(summed.astype(jnp.bfloat16), (1, 0, 2)).reshape(
            QBLK, head_group * HEAD_SIZE
        )

    head_out = lax.map(output_block, block_ids).reshape(seq_len, head_group * HEAD_SIZE)
    grad_tok = grad_out[0]
    tok_out = lax.all_to_all(head_out, "seq", split_axis=0, concat_axis=1, tiled=True)
    tok_grad = lax.dot_general(
        grad_tok,
        lax.all_gather(out_weight, ("seq", "dp"), axis=0, tiled=True),
        (((1,), (1,)), ((), ())),
        preferred_element_type=jnp.float32,
    ).astype(jnp.bfloat16)
    columns = tok_out
    seq_part = lax.psum_scatter(
        lax.dot_general(
            columns, grad_tok, (((0,), (0,)), ((), ())), preferred_element_type=jnp.float32
        ).astype(jnp.bfloat16),
        "seq",
        scatter_dimension=0,
        tiled=True,
    )
    head_grad = lax.all_to_all(tok_grad, "seq", split_axis=1, concat_axis=0, tiled=True)
    weight_grad = (
        lax.psum_scatter(seq_part, "dp", scatter_dimension=0, tiled=True).astype(jnp.float32)
        * grad_scale
    )
    grad_blocks = head_grad.reshape(query_blocks, QBLK, head_group, HEAD_SIZE)
    out_blocks = head_out.reshape(query_blocks, QBLK, head_group, HEAD_SIZE)

    def backward_block(state, q_index):
        key_sum, value_sum = state
        q_block = q_blocks[q_index]
        g_block = grad_blocks[q_index]
        row_lse = log_totals[q_index]
        delta = jnp.einsum(
            "qgd,qgd->gq", g_block, out_blocks[q_index], preferred_element_type=jnp.float32
        )

        def backward_advance(k_index, inner):
            query_sum, key_sum, value_sum = inner
            masked, allowed, k_block = block_scores(q_block, q_index, k_index)
            v_block = lax.dynamic_slice_in_dim(head_v, k_index * QBLK, QBLK, 0)
            weights = jnp.where(allowed[None], jnp.exp(masked - row_lse[:, :, None]), 0.0)
            dweights = jnp.einsum(
                "qgd,kd->gqk", g_block, v_block, preferred_element_type=jnp.float32
            )
            dscores = (weights * (dweights - delta[:, :, None])).astype(jnp.bfloat16)
            query_sum = query_sum + jnp.einsum(
                "gqk,kd->gqd", dscores, k_block, preferred_element_type=jnp.float32
            )
            key_piece = jnp.einsum(
                "gqk,qgd->kd", dscores, q_block, preferred_element_type=jnp.float32
            )
            value_piece = jnp.einsum(
                "gqk,qgd->kd",
                weights.astype(jnp.bfloat16),
                g_block,
                preferred_element_type=jnp.float32,
            )
            key_old = lax.dynamic_slice_in_dim(key_sum, k_index * QBLK, QBLK, 0)
            value_old = lax.dynamic_slice_in_dim(value_sum, k_index * QBLK, QBLK, 0)
            key_sum = lax.dynamic_update_slice_in_dim(
                key_sum, key_old + key_piece, k_index * QBLK, 0
            )
            value_sum = lax.dynamic_update_slice_in_dim(
                value_sum, value_old + value_piece, k_index * QBLK, 0
            )
            return (query_sum, key_sum, value_sum)

        start_inner = (jnp.zeros((head_group, QBLK, HEAD_SIZE), jnp.float32), key_sum, value_sum)
        query_sum, key_sum, value_sum = lax.fori_loop(
            key_starts[q_index], q_index + 1, backward_advance, start_inner
        )
        dq_block = jnp.transpose((query_sum * soft_scale).astype(jnp.bfloat16), (1, 0, 2)).reshape(
            QBLK, head_group * HEAD_SIZE
        )
        return ((key_sum, value_sum), dq_block)

    start_sums = (
        jnp.zeros((seq_len, HEAD_SIZE), jnp.float32),
        jnp.zeros((seq_len, HEAD_SIZE), jnp.float32),
    )
    (key_sum, value_sum), dq_blocks = lax.scan(backward_block, start_sums, block_ids)
    head_dq = dq_blocks.reshape(seq_len, head_group * HEAD_SIZE)
    key_part = (key_sum * soft_scale).astype(jnp.bfloat16)
    value_part = value_sum.astype(jnp.bfloat16)
    back_q, back_k, back_v = (
        lax.all_to_all(head_dq, "seq", split_axis=0, concat_axis=1, tiled=True),
        lax.all_to_all(key_part, "seq", split_axis=0, concat_axis=1, tiled=True),
        lax.all_to_all(value_part, "seq", split_axis=0, concat_axis=1, tiled=True),
    )

    def merge_groups(back_rows):
        split_groups = back_rows.reshape(tok_dev, kv_heads, repeat_count, HEAD_SIZE).astype(
            jnp.float32
        )
        return (
            jnp.sum(split_groups, axis=2)
            .astype(jnp.bfloat16)
            .reshape(tok_dev, kv_heads * HEAD_SIZE)
        )

    dk_tok = merge_groups(back_k)
    dv_tok = merge_groups(back_v)

    def to_sources(packed_rows):
        columns = packed_rows.shape[1]
        head_grouped = packed_rows.reshape(block_count, PACK, columns)
        picked = jnp.take(head_grouped, jnp.minimum(landing, block_count - 1), axis=0)
        return picked

    ret_q, ret_k, ret_v = (
        lax.all_to_all(to_sources(back_q), "dp", split_axis=0, concat_axis=0, tiled=True),
        lax.all_to_all(to_sources(dk_tok), "dp", split_axis=0, concat_axis=0, tiled=True),
        lax.all_to_all(to_sources(dv_tok), "dp", split_axis=0, concat_axis=0, tiled=True),
    )

    def to_samples(returned):
        columns = returned.shape[2]
        return jnp.take(returned, send_index, axis=0).reshape(tok_dev, columns)

    return (to_samples(ret_q), to_samples(ret_k), to_samples(ret_v), weight_grad)


def solution(mesh):
    return jax.shard_map(
        body,
        mesh=mesh,
        in_specs=(
            P(("seq", "dp"), None),
            P(("seq", "dp"), None),
            P(("seq", "dp"), None),
            P(("seq", "dp")),
            P(("seq", "dp")),
            P("dp", None),
            P("dp", "seq", None),
            P(("seq", "dp"), None),
        ),
        out_specs=(
            P(("seq", "dp"), None),
            P(("seq", "dp"), None),
            P(("seq", "dp"), None),
            P(("seq", "dp"), None),
        ),
        check_vma=False,
    )
```

profile of v0, /device:TPU:65, one launch (start us, length us, event | category | flops | bytes accessed | tf_op | source)
XLA Modules:
  0.0 576.4 jit_solution(11790713067474264996)
XLA Ops:
  11.6 10.2 %all-to-all-start = ((bf16[32,1,1]{2,1,0:T(2,128)(2,1)}), bf16[32,1,1]{2,1,0:T(2,128)(2,1)S(1)}, u32[]{:S(2)}, u32[]{:S(2)}) async-start(bf16[32,1,1]{2,1,0:T(2,128)(2,1)} %copy.81), calls=%async_computation | async-start | bytes 32768 | tf_op jit(solution)/shard_map/all_to_all | solution.py:46
  22.5 2.4 scatter_fusion.2
  24.9 3.6 all-to-all-done
  28.6 5.6 all-to-all-start.3
  35.3 2.6 scatter_fusion
  37.9 5.7 all-to-all-done.3
  43.5 5.0 all-to-all-start.1
  49.2 2.2 scatter_fusion.4
  51.4 20.5 %all-to-all-done.1 = bf16[32,8,2048]{2,1,0:T(8,128)(2,1)S(1)} async-done(((bf16[32,8,2048]{2,1,0:T(8,128)(2,1)}), bf16[32,8,2048]{2,1,0:T(8,128)(2,1)S(1)}, u32[]{:S(2)}, u32[]{:S(2)}) %all-to-all-start.1) | async-done | bytes 1048608 | tf_op jit(solution)/shard_map/all_to_all | solution.py:43
  71.9 7.0 %all-to-all-start.6 = ((bf16[32,8,512]{2,1,0:T(8,128)(2,1)}), bf16[32,8,512]{2,1,0:T(8,128)(2,1)S(1)}, u32[]{:S(2)}, u32[]{:S(2)}) async-start(bf16[32,8,512]{2,1,0:T(8,128)(2,1)} %scatter_fusion.4), calls=%async_computation.6 | async-start | bytes 524288 | tf_op jit(solution)/shard_map/all_to_all | solution.py:45
  80.8 1.6 scatter_fusion.1
  83.5 4.8 all-to-all-done.6
  88.3 9.6 %all-to-all-start.2 = ((bf16[128,8,256]{2,0,1:T(8,128)(2,1)}), bf16[128,8,256]{2,0,1:T(8,128)(2,1)S(1)}, u32[]{:S(2)}, u32[]{:S(2)}) async-start(bf16[128,8,256]{2,0,1:T(8,128)(2,1)} %copy.83), calls=%async_computation.2 | async-start | bytes 1048576 | tf_op jit(solution)/shard_map/all_to_all | solution.py:65
  101.6 5.8 %all-to-all-done.2 = bf16[128,8,256]{2,0,1:T(8,128)(2,1)S(1)} async-done(((bf16[128,8,256]{2,0,1:T(8,128)(2,1)}), bf16[128,8,256]{2,0,1:T(8,128)(2,1)S(1)}, u32[]{:S(2)}, u32[]{:S(2)}) %all-to-all-start.2) | async-done | bytes 524320 | tf_op jit(solution)/shard_map/all_to_all | solution.py:65
  108.2 4.2 all-to-all-start.4
  115.2 3.7 all-to-all-done.4
  119.7 4.4 all-to-all-start.7
  124.0 19.3 %while.92 = (s32[]{:T(128)}, f32[2,2,512]{2,1,0:T(2,128)S(1)}, s32[2]{0:T(128)S(1)}, s32[2]{0:T(128)S(1)}, bf16[2,512,2,128]{3,1,2,0:T(8,128)(2,1)}, /*index=5*/...) while((s32[]{:T(128)}, f32[2,2,512]{2,1,0:T(2,128)S(1)}, ...), condition=%wide.region_12.13_spmd.clone.clone, body=%wide.region_7.12_spmd.clone.clone.sunk | while | flops 139202576 | bytes 5997168 | solution.py:112
  129.1 4.6 while.97
  138.8 4.6 while.97
  144.2 22.9 %while.94 = (s32[]{:T(128)}, bf16[2,512,256]{2,1,0:T(8,128)(2,1)}, s32[2]{0:T(128)S(1)}, s32[2]{0:T(128)S(1)}, bf16[2,512,2,128]{3,1,2,0:T(8,128)(2,1)}, /*index...) while((s32[]{:T(128)}, bf16[2,512,256]{2,1,0:T(8,128)(2,1)}, ...), condition=%wide.region_18.19_spmd.clone.clone, body=%wide.region_15.18_spmd.clone.clone.sunk | while | flops 272106496 | bytes 5543548 | solution.py:138
  149.7 4.7 while.98
  161.2 4.7 while.98
  167.2 4.8 all-to-all-start.14
  172.0 2.0 reshape_reshape.19
  174.0 7.5 %all-to-all-done.14 = bf16[8,128,256]{2,1,0:T(8,128)(2,1)S(1)} async-done(((bf16[8,128,256]{2,1,0:T(8,128)(2,1)}), bf16[8,128,256]{2,1,0:T(8,128)(2,1)S(1)}, u32[]{:S(2)}, u32[]{:S(2)}) %all-to-all-start.14) | async-done | bytes 524320 | tf_op jit(solution)/shard_map/all_to_all | solution.py:140
  181.7 34.5 %all-gather.2.cloned.1.call-done = bf16[2048,2048]{1,0:T(8,128)(2,1)} async-done(((bf16[8,2048]{1,0:T(8,128)(2,1)}), bf16[2048,2048]{1,0:T(8,128)(2,1)}) %all-gather.2.cloned.1.call-update) | async-done | bytes 8388624 | tf_op jit(solution)/shard_map/all_gather | solution.py:143
  216.2 6.3 %convolution_convert_fusion.1 = bf16[128,2048]{1,0:T(8,128)(2,1)S(1)} fusion(bf16[2048,2048]{1,0:T(8,128)(2,1)} %all-gather.2.cloned.1.call-done, bf16[1,128,2048]{2,1,0:T(8,128)(2,1)S(1)} %copy-done), kind=kOutput, calls=%fused_computation.93 | convolution fusion | flops 1074003968 | bytes 9437184 | tf_op jit(solution)/shard_map/dot_general | solution.py:141
  223.3 4.5 all-to-all-start.5
  227.8 5.5 convolution_convert_fusion
  233.4 3.9 all-to-all-done.5
  239.1 31.8 %while.96 = (s32[]{:T(128)}, f32[1024,128]{1,0:T(8,128)S(1)}, f32[1024,128]{1,0:T(8,128)S(1)}, bf16[2,512,256]{2,1,0:T(8,128)(2,1)}, s32[2]{0:T(128)S(1)}, /*ind...) while((s32[]{:T(128)}, f32[1024,128]{1,0:T(8,128)S(1)}, ...), condition=%wide.region_22.23_spmd.clone.clone, body=%wide.region_19.22_spmd.clone.clone.sunk | while | flops 677117952 | bytes 19321592 | solution.py:217
  245.9 1.6 multiply_reduce_fusion.2
  247.6 6.2 %while.99 = (s32[]{:T(128)}, f32[2,512,128]{2,1,0:T(8,128)S(1)}, f32[1024,128]{1,0:T(8,128)S(1)}, f32[1024,128]{1,0:T(8,128)S(1)}, s32[]{:T(128)}, /*index=5*/s3...) while((s32[]{:T(128)}, f32[2,512,128]{2,1,0:T(8,128)S(1)}, ...), condition=%wide.region_21.21_spmd.clone, body=%wide.region_20.20_spmd.clone.sunk | while | flops 676332544 | bytes 13527291 | solution.py:205
  261.8 1.6 multiply_reduce_fusion.2
  263.5 6.2 %while.99 = (s32[]{:T(128)}, f32[2,512,128]{2,1,0:T(8,128)S(1)}, f32[1024,128]{1,0:T(8,128)S(1)}, f32[1024,128]{1,0:T(8,128)S(1)}, s32[]{:T(128)}, /*index=5*/s3...) while((s32[]{:T(128)}, f32[2,512,128]{2,1,0:T(8,128)S(1)}, ...), condition=%wide.region_21.21_spmd.clone, body=%wide.region_20.20_spmd.clone.sunk | while | flops 676332544 | bytes 13527291 | solution.py:205
  271.7 4.2 all-to-all-start.10
  276.6 7.7 %all-to-all-done.10 = bf16[8,128,128]{2,1,0:T(8,128)(2,1)S(1)} async-done(((bf16[8,128,128]{2,1,0:T(8,128)(2,1)}), bf16[8,128,128]{2,1,0:T(8,128)(2,1)S(1)}, u32[]{:S(2)}, u32[]{:S(2)}) %all-to-all-start.10) | async-done | bytes 262176 | tf_op jit(solution)/shard_map/all_to_all | solution.py:223
  284.3 4.2 all-to-all-start.12
  288.5 6.5 %all-to-all-done.12 = bf16[8,128,128]{2,1,0:T(8,128)(2,1)S(1)} async-done(((bf16[8,128,128]{2,1,0:T(8,128)(2,1)}), bf16[8,128,128]{2,1,0:T(8,128)(2,1)S(1)}, u32[]{:S(2)}, u32[]{:S(2)}) %all-to-all-start.12) | async-done | bytes 262176 | tf_op jit(solution)/shard_map/all_to_all | solution.py:224
  295.0 4.4 all-to-all-start.8
  301.9 7.1 %all-to-all-done.8 = bf16[8,128,256]{2,1,0:T(8,128)(2,1)S(1)} async-done(((bf16[8,128,256]{2,1,0:T(8,128)(2,1)}), bf16[8,128,256]{2,1,0:T(8,128)(2,1)S(1)}, u32[]{:S(2)}, u32[]{:S(2)}) %all-to-all-start.8) | async-done | bytes 524320 | tf_op jit(solution)/shard_map/all_to_all | solution.py:222
  308.9 22.8 %all_to_all.176 = bf16[32,8,512]{2,1,0:T(8,128)(2,1)S(1)} all-to-all(bf16[32,8,512]{2,1,0:T(8,128)(2,1)S(1)} %get-tuple-element.1148), channel_id=1, replica_groups=mesh['seq'=8,'dp'=32] {'dp'}, dimensions={0} | all-to-all | bytes 524288 | tf_op jit(solution)/shard_map/all_to_all | solution.py:249
  331.7 5.5 all-to-all-start.11
  339.5 7.3 %all-to-all-done.11 = bf16[32,8,512]{2,1,0:T(8,128)(2,1)S(1)} async-done(((bf16[32,8,512]{2,1,0:T(8,128)(2,1)}), bf16[32,8,512]{2,1,0:T(8,128)(2,1)S(1)}, u32[]{:S(2)}, u32[]{:S(2)}) %all-to-all-start.11) | async-done | bytes 262176 | tf_op jit(solution)/shard_map/all_to_all | solution.py:248
  346.8 5.4 all-to-all-start.9
  354.9 21.2 %all-to-all-done.9 = bf16[32,8,2048]{2,1,0:T(8,128)(2,1)S(1)} async-done(((bf16[32,8,2048]{2,1,0:T(8,128)(2,1)}), bf16[32,8,2048]{2,1,0:T(8,128)(2,1)S(1)}, u32[]{:S(2)}, u32[]{:S(2)}) %all-to-all-start.9) | async-done | bytes 1048608 | tf_op jit(solution)/shard_map/all_to_all | solution.py:247
  377.6 190.0 %reduce-scatter.5.cloned.1.call-done = bf16[8,2048]{1,0:T(8,128)(2,1)} async-done(((bf16[256,2048]{1,0:T(8,128)(2,1)}), bf16[8,2048]{1,0:T(8,128)(2,1)}) %reduce-scatter.5.cloned.1.call-update) | async-done | bytes 32784 | tf_op jit(solution)/shard_map/reduce_scatter | solution.py:158
  (201 shorter events, 65.7 us)
Async XLA Ops:
  8.0 208.2 %copy-start = (bf16[1,128,2048]{2,1,0:T(8,128)(2,1)S(1)}, bf16[1,128,2048]{2,1,0:T(8,128)(2,1)}, u32[]{:S(2)}) copy-start(bf16[1,128,2048]{2,1,0:T(8,128)(2,1)} %param.30) | copy-start | bytes 1572868
  8.0 27.3 %copy-start.2 = (bf16[128,2048]{1,0:T(8,128)(2,1)S(1)}, bf16[128,2048]{1,0:T(8,128)(2,1)}, u32[]{:S(2)}) copy-start(bf16[128,2048]{1,0:T(8,128)(2,1)} %param.24) | copy-start | bytes 1572868
  10.1 39.1 %copy-start.4 = (s32[16]{0:T(128)}, s32[16]{0:T(128)S(1)}, u32[]{:S(2)}) copy-start(s32[16]{0:T(128)S(1)} %get-tuple-element.1134) | copy-start | bytes 196
  11.6 16.9 %all-to-all-start = ((bf16[32,1,1]{2,1,0:T(2,128)(2,1)}), bf16[32,1,1]{2,1,0:T(2,128)(2,1)S(1)}, u32[]{:S(2)}, u32[]{:S(2)}) async-start(bf16[32,1,1]{2,1,0:T(2,128)(2,1)} %copy.81), calls=%async_computation | async-start | bytes 32768 | tf_op jit(solution)/shard_map/all_to_all | solution.py:46
  28.6 15.0 %all-to-all-start.3 = ((bf16[32,8,512]{2,1,0:T(8,128)(2,1)}), bf16[32,8,512]{2,1,0:T(8,128)(2,1)S(1)}, u32[]{:S(2)}, u32[]{:S(2)}) async-start(bf16[32,8,512]{2,1,0:T(8,128)(2,1)} %scatter_fusion.2), calls=%async_computation.3 | async-start | bytes 524288 | tf_op jit(solution)/shard_map/all_to_all | solution.py:44
  35.3 14.0 %copy-start.3 = (bf16[128,512]{1,0:T(8,128)(2,1)S(1)}, bf16[128,512]{1,0:T(8,128)(2,1)}, u32[]{:S(2)}) copy-start(bf16[128,512]{1,0:T(8,128)(2,1)} %param.26) | copy-start | bytes 393220
  43.5 28.4 %all-to-all-start.1 = ((bf16[32,8,2048]{2,1,0:T(8,128)(2,1)}), bf16[32,8,2048]{2,1,0:T(8,128)(2,1)S(1)}, u32[]{:S(2)}, u32[]{:S(2)}) async-start(bf16[32,8,2048]{2,1,0:T(8,128)(2,1)} %scatter_fusion), calls=%async_computation.1 | async-start | bytes 2097152 | tf_op jit(solution)/shard_map/all_to_all | solution.py:43
  71.9 16.4 %all-to-all-start.6 = ((bf16[32,8,512]{2,1,0:T(8,128)(2,1)}), bf16[32,8,512]{2,1,0:T(8,128)(2,1)S(1)}, u32[]{:S(2)}, u32[]{:S(2)}) async-start(bf16[32,8,512]{2,1,0:T(8,128)(2,1)} %scatter_fusion.4), calls=%async_computation.6 | async-start | bytes 524288 | tf_op jit(solution)/shard_map/all_to_all | solution.py:45
  82.5 16.8 %copy-start.1 = (s32[1,1024]{1,0:T(1,128)S(1)}, s32[1,1024]{1,0:T(1,128)}, u32[]{:S(2)}) copy-start(s32[1,1024]{1,0:T(1,128)} %param.29) | copy-start | bytes 12292
  88.3 19.1 %all-to-all-start.2 = ((bf16[128,8,256]{2,0,1:T(8,128)(2,1)}), bf16[128,8,256]{2,0,1:T(8,128)(2,1)S(1)}, u32[]{:S(2)}, u32[]{:S(2)}) async-start(bf16[128,8,256]{2,0,1:T(8,128)(2,1)} %copy.83), calls=%async_computation.2 | async-start | bytes 1048576 | tf_op jit(solution)/shard_map/all_to_all | solution.py:65
  98.0 118.2 %all-gather.2.cloned.1.call-start = ((), (), s32[]{:S(2)}) async-start(), calls=%async_computation.17 | async-start | bytes 8421376 | tf_op jit(solution)/shard_map/all_gather | solution.py:143
  108.2 10.8 %all-to-all-start.4 = ((bf16[128,8,128]{2,0,1:T(8,128)(2,1)}), bf16[128,8,128]{2,0,1:T(8,128)(2,1)S(1)}, u32[]{:S(2)}, u32[]{:S(2)}) async-start(bf16[128,8,128]{2,0,1:T(8,128)(2,1)} %bitcast.9), calls=%async_computation.4 | async-start | bytes 524288 | tf_op jit(solution)/shard_map/all_to_all | solution.py:66
  119.7 23.7 %all-to-all-start.7 = ((bf16[128,8,128]{2,0,1:T(8,128)(2,1)}), bf16[128,8,128]{2,0,1:T(8,128)(2,1)S(1)}, u32[]{:S(2)}, u32[]{:S(2)}) async-start(bf16[128,8,128]{2,0,1:T(8,128)(2,1)} %bitcast.16), calls=%async_computation.7 | async-start | bytes 524288 | tf_op jit(solution)/shard_map/all_to_all | solution.py:67
  167.2 14.3 %all-to-all-start.14 = ((bf16[8,128,256]{2,1,0:T(8,128)(2,1)}), bf16[8,128,256]{2,1,0:T(8,128)(2,1)S(1)}, u32[]{:S(2)}, u32[]{:S(2)}) async-start(bf16[8,128,256]{2,1,0:T(8,128)(2,1)} %bitcast.31), calls=%async_computation.14 | async-start | bytes 1048576 | tf_op jit(solution)/shard_map/all_to_all | solution.py:140
  223.3 14.0 %all-to-all-start.5 = ((bf16[128,8,256]{2,0,1:T(8,128)(2,1)}), bf16[128,8,256]{2,0,1:T(8,128)(2,1)S(1)}, u32[]{:S(2)}, u32[]{:S(2)}) async-start(bf16[128,8,256]{2,0,1:T(8,128)(2,1)} %bitcast.163), calls=%async_computation.5 | async-start | bytes 1048576 | tf_op jit(solution)/shard_map/all_to_all | solution.py:156
  227.8 124.5 %reduce-scatter.3.cloned.1.call-start = ((), (), s32[]{:S(2)}) async-start(), calls=%async_computation.18 | async-start | bytes 9437184 | tf_op jit(solution)/shard_map/reduce_scatter | solution.py:148
  239.1 36.7 %copy-start.8 = (s32[32]{0:T(128)S(1)}, s32[32]{0:T(128)}, u32[]{:S(2)}) copy-start(s32[32]{0:T(128)} %get-tuple-element.1001) | copy-start | bytes 388
  271.7 12.6 %all-to-all-start.10 = ((bf16[8,128,128]{2,1,0:T(8,128)(2,1)}), bf16[8,128,128]{2,1,0:T(8,128)(2,1)S(1)}, u32[]{:S(2)}, u32[]{:S(2)}) async-start(bf16[8,128,128]{2,1,0:T(8,128)(2,1)} %bitcast.23), calls=%async_computation.10 | async-start | bytes 524288 | tf_op jit(solution)/shard_map/all_to_all | solution.py:223
  284.3 10.7 %all-to-all-start.12 = ((bf16[8,128,128]{2,1,0:T(8,128)(2,1)}), bf16[8,128,128]{2,1,0:T(8,128)(2,1)S(1)}, u32[]{:S(2)}, u32[]{:S(2)}) async-start(bf16[8,128,128]{2,1,0:T(8,128)(2,1)} %bitcast.27), calls=%async_computation.12 | async-start | bytes 524288 | tf_op jit(solution)/shard_map/all_to_all | solution.py:224
  295.0 13.9 %all-to-all-start.8 = ((bf16[8,128,256]{2,1,0:T(8,128)(2,1)}), bf16[8,128,256]{2,1,0:T(8,128)(2,1)S(1)}, u32[]{:S(2)}, u32[]{:S(2)}) async-start(bf16[8,128,256]{2,1,0:T(8,128)(2,1)} %bitcast.19), calls=%async_computation.8 | async-start | bytes 1048576 | tf_op jit(solution)/shard_map/all_to_all | solution.py:222
  299.6 37.6 %copy-start.7 = (s32[32]{0:T(128)S(1)}, s32[32]{0:T(128)}, u32[]{:S(2)}) copy-start(s32[32]{0:T(128)} %get-tuple-element.1150) | copy-start | bytes 388
  331.7 15.2 %all-to-all-start.11 = ((bf16[32,8,512]{2,1,0:T(8,128)(2,1)}), bf16[32,8,512]{2,1,0:T(8,128)(2,1)S(1)}, u32[]{:S(2)}, u32[]{:S(2)}) async-start(bf16[32,8,512]{2,1,0:T(8,128)(2,1)} %get-tuple-element.1149), calls=%async_computation.11 | async-start | bytes 524288 | tf_op jit(solution)/shard_map/all_to_all | solution.py:248
  339.5 13.3 %copy-start.6 = (pred[16]{0:T(512)(128)(4,1)S(1)}, pred[16]{0:T(512)(128)(4,1)}, u32[]{:S(2)}) copy-start(pred[16]{0:T(512)(128)(4,1)} %get-tuple-element.1133) | copy-start | bytes 52
  339.5 13.5 %copy-start.5 = (s32[16]{0:T(128)S(1)}, s32[16]{0:T(128)}, u32[]{:S(2)}) copy-start(s32[16]{0:T(128)} %copy-done.4) | copy-start | bytes 196
  346.8 29.3 %all-to-all-start.9 = ((bf16[32,8,2048]{2,1,0:T(8,128)(2,1)}), bf16[32,8,2048]{2,1,0:T(8,128)(2,1)S(1)}, u32[]{:S(2)}, u32[]{:S(2)}) async-start(bf16[32,8,2048]{2,1,0:T(8,128)(2,1)} %broadcast_select_fusion), calls=%async_computation.9 | async-start | bytes 2097152 | tf_op jit(solution)/shard_map/all_to_all | solution.py:247
  352.2 215.4 %reduce-scatter.5.cloned.1.call-start = ((), (), s32[]{:S(2)}) async-start(), calls=%async_computation.19 | async-start | bytes 1081344 | tf_op jit(solution)/shard_map/reduce_scatter | solution.py:158
Sparse Core Ops, SparseCore 0:
  102.5 113.6 all-gather.1
Sparse Core Ops, SparseCore 1:
  233.5 56.0 reduce-scatter.2
  356.5 211.0 reduce-scatter.4
where the time goes:
time: 585 us; the launch traced here: 576 us
  waiting for transfers between devices  331 us (57%)
  starting transfers between devices  79 us (14%)
  local copies, waits for them, and re-layouts  49.7 us (8%)
  loops' own time  37.5 us (6%)
  blocking collectives  22.8 us (4%)
  matrix products  20.7 us (4%)
  other arithmetic  19.8 us (3%)
  between operations  15.9 us (3%)
    reduce_scatter x1, waiting for transfers between devices, body(): lax.psum_scatter(seq_part, 'dp', scatter_dimension=0, tiled=True)  190 us
    all_gather x1, waiting for transfers between devices, body(): lax.all_gather(out_weight, ('seq', 'dp'), axis=0, tiled=True)  34.5 us
    all_to_all x1, blocking collectives, body(): lax.all_to_all(to_sources(dv_tok), 'dp', split_axis=0, concat_axis=0, til...  22.8 us
    all_to_all x1, waiting for transfers between devices, body(): lax.all_to_all(to_sources(back_q), 'dp', split_axis=0, concat_axis=0, til...  21.2 us
    all_to_all x1, waiting for transfers between devices, body(): lax.all_to_all(to_slots(q_rows), 'dp', split_axis=0, concat_axis=0, tiled...  20.5 us
  transfers between devices with their start and end apart: 17, of which 15 were waited for; matrix products, arithmetic and copies ran while one was open for 14% of the time, Pallas kernels for 0%

commit v1 on v0

v1 whole, which is shorter than its diff:
```python
import math

import jax
import jax.numpy as jnp
from jax import lax
from jax.experimental import pallas as pl
from jax.experimental.pallas import tpu as pltpu
from jax.sharding import PartitionSpec as P

HEAD = 128
PACK = 8
NEG_FILL = -1e30
MESH = pl.DeviceIdType.MESH
BF16 = jnp.bfloat16
F32 = jnp.float32
N_SEQ, N_Y = 8, 4
N_DP, N_Z, N_X = 32, 8, 4
TOK = 128
SEQ_LEN = 1024
D = 2048
KV_COLS = 1024
QB = 256
SOFT_SCALE = 1.0 / math.sqrt(HEAD)
GRAD_SCALE = 8.0 / math.sqrt(N_DP * SEQ_LEN)
VMEM = pl.BlockSpec(memory_space=pltpu.VMEM)


def nn(a, b):
    return lax.dot_general(a, b, (((1,), (0,)), ((), ())), preferred_element_type=F32)


def nt(a, b):
    return lax.dot_general(a, b, (((1,), (1,)), ((), ())), preferred_element_type=F32)


def remote(src, dst, send, recv, seq, dp):
    return pltpu.make_async_remote_copy(
        src_ref=src, dst_ref=dst, send_sem=send, recv_sem=recv, device_id=(seq, dp), device_id_type=MESH
    )


def greet(s, d):
    barrier = pltpu.get_barrier_semaphore()

    def along_dp(i, carry):
        pl.semaphore_signal(barrier, inc=1, device_id=(s, lax.rem(d + i, N_DP)), device_id_type=MESH)
        return carry

    def along_seq(i, carry):
        pl.semaphore_signal(barrier, inc=1, device_id=(lax.rem(s + i, N_SEQ), d), device_id_type=MESH)
        return carry

    lax.fori_loop(1, N_DP, along_dp, 0)
    lax.fori_loop(1, N_SEQ, along_seq, 0)
    return barrier


def wait_greeted(barrier):
    pl.semaphore_wait(barrier, N_DP - 1 + N_SEQ - 1)


def send_slots(slots, came, send, recv, s, d):
    def one(i, carry):
        p = lax.rem(d + i, N_DP)
        remote(slots.at[p], came.at[d], send, recv, s, p).start()
        return carry

    lax.fori_loop(1, N_DP, one, 0)


def wait_bytes(ref, sem):
    pltpu.make_async_copy(ref, ref, sem).wait()


def slot_rows(ref, columns):
    block = ref[:, :, columns]
    return block.astype(F32).reshape(N_DP * PACK, block.shape[2]).astype(BF16)


def as_slots(rows):
    return rows.reshape(N_DP, PACK, rows.shape[1]).astype(BF16)


def forward_exchange(
    q_ref, k_ref, v_ref, target_ref, landing_ref, grad_ref, w_ref,
    q_all, k_all, v_all, came_tag, g_all, w_all,
    slots_t, slots_kv, slots_q, came_kv, came_q, packed_kv, packed_q,
    own, slot_send, slot_recv, head_send, head_recv, g_send, g_recv, w_send, w_recv,
):
    s, d = lax.axis_index("seq"), lax.axis_index("dp")
    y, core = s // 2, lax.rem(s, 2)
    z, x = d // N_X, lax.rem(d, N_X)
    mate = y * 2 + 1 - core
    up, down = lax.rem(y + 1, N_Y) * 2 + core, lax.rem(y + N_Y - 1, N_Y) * 2 + core
    across = lax.rem(y + 2, N_Y) * 2 + core
    barrier = greet(s, d)

    own_g = pltpu.make_async_copy(grad_ref, g_all.at[s], own.at[0])
    own_w = pltpu.make_async_copy(w_ref, w_all.at[z, x], own.at[1])
    own_g.start()
    own_w.start()

    place = (lax.broadcasted_iota(jnp.int32, (N_DP * PACK, TOK), 0) == target_ref[...]).astype(F32).astype(BF16)
    tags = (lax.broadcasted_iota(jnp.int32, (TOK, TOK), 1) == landing_ref[...]).astype(F32).astype(BF16)
    slots_t[...] = as_slots(nn(place, tags))
    for part, ref in enumerate((k_ref, v_ref)):
        for c in range(2):
            cols = slice(part * 512 + c * 256, part * 512 + (c + 1) * 256)
            slots_kv[:, :, cols] = as_slots(nn(place, ref[:, c * 256 : (c + 1) * 256]))
    own_g.wait()
    own_w.wait()
    wait_greeted(barrier)

    g_up = remote(g_all.at[s], g_all.at[s], g_send.at[0], g_recv.at[0], up, d)
    g_down = remote(g_all.at[s], g_all.at[s], g_send.at[1], g_recv.at[1], down, d)
    g_mate = remote(g_all.at[s], g_all.at[s], g_send.at[2], g_recv.at[2], mate, d)
    send_slots(slots_t, came_tag, slot_send.at[0], slot_recv.at[0], s, d)
    g_up.start()
    g_down.start()
    g_mate.start()

    def weight_z(i, carry):
        zz = lax.rem(z + i, N_Z)
        remote(w_all.at[z, x], w_all.at[z, x], w_send.at[0], w_recv.at[0], s, zz * N_X + x).start()
        return carry

    lax.fori_loop(1, N_Z, weight_z, 0)
    send_slots(slots_kv, came_kv, slot_send.at[1], slot_recv.at[1], s, d)

    for g in range(N_SEQ):
        both = nn(place, q_ref[:, g * 256 : (g + 1) * 256])
        slots_q[0, :, :, g * HEAD : (g + 1) * HEAD] = as_slots(both[:, :HEAD])
        slots_q[1, :, :, g * HEAD : (g + 1) * HEAD] = as_slots(both[:, HEAD:])
    for h in range(2):
        send_slots(slots_q.at[h], came_q.at[h], slot_send.at[2 + h], slot_recv.at[2 + h], s, d)

    kept = [
        pltpu.make_async_copy(slots_t.at[d], came_tag.at[d], own.at[0]),
        pltpu.make_async_copy(slots_kv.at[d], came_kv.at[d], own.at[1]),
        pltpu.make_async_copy(slots_q.at[0, d], came_q.at[0, d], own.at[2]),
        pltpu.make_async_copy(slots_q.at[1, d], came_q.at[1, d], own.at[3]),
    ]
    for copy in kept:
        copy.start()
    for copy in kept:
        copy.wait()

    wait_bytes(w_all.at[0 : N_Z - 1, 0], w_recv.at[0])
    wait_bytes(w_all.at[0 : N_Z - 1, 0], w_send.at[0])

    def weight_x(i, carry):
        xx = lax.rem(x + i, N_X)
        remote(w_all.at[:, x], w_all.at[:, x], w_send.at[1], w_recv.at[1], s, z * N_X + xx).start()
        return carry

    lax.fori_loop(1, N_X, weight_x, 0)

    g_up.wait_recv()
    from_down = g_all.at[down]
    half_up = remote(from_down.at[0:64], from_down.at[0:64], g_send.at[3], g_recv.at[3], up, d)
    mate_down = remote(from_down, from_down, g_send.at[4], g_recv.at[4], mate, d)
    half_up.start()
    mate_down.start()
    g_down.wait_recv()
    from_up = g_all.at[up]
    half_down = remote(from_up.at[64:128], from_up.at[64:128], g_send.at[5], g_recv.at[5], down, d)
    mate_up = remote(from_up, from_up, g_send.at[6], g_recv.at[6], mate, d)
    half_down.start()
    mate_up.start()

    wait_bytes(came_tag.at[0 : N_DP - 1], slot_recv.at[0])
    tag_rows = came_tag[...].astype(F32).reshape(N_DP * PACK, TOK)
    gather = tag_rows.T.astype(BF16)
    wait_bytes(came_kv.at[0 : N_DP - 1], slot_recv.at[1])
    for c in range(4):
        two = nn(gather, slot_rows(came_kv, slice(c * 256, (c + 1) * 256))).astype(BF16)
        packed_kv[2 * c] = two[:, :HEAD]
        packed_kv[2 * c + 1] = two[:, HEAD:]

    def keys_out(i, carry):
        t = lax.rem(s + i, N_SEQ)
        remote(packed_kv.at[t // 2], k_all.at[s], head_send.at[0], head_recv.at[0], t, d).start()
        remote(packed_kv.at[4 + t // 2], v_all.at[s], head_send.at[1], head_recv.at[1], t, d).start()
        return carry

    lax.fori_loop(1, N_SEQ, keys_out, 0)
    kept = [
        pltpu.make_async_copy(packed_kv.at[s // 2], k_all.at[s], own.at[0]),
        pltpu.make_async_copy(packed_kv.at[4 + s // 2], v_all.at[s], own.at[1]),
    ]
    for copy in kept:
        copy.start()

    half_up.wait_recv()
    half_down.wait_recv()
    from_across = g_all.at[across]
    mate_across = remote(from_across, from_across, g_send.at[7], g_recv.at[7], mate, d)
    mate_across.start()

    for h in range(2):
        wait_bytes(came_q.at[h, 0 : N_DP - 1], slot_recv.at[2 + h])
        for c in range(4):
            two = nn(gather, slot_rows(came_q.at[h], slice(c * 256, (c + 1) * 256))).astype(BF16)
            packed_q[h, 2 * c] = two[:, :HEAD]
            packed_q[h, 2 * c + 1] = two[:, HEAD:]

        def queries_out(i, carry):
            t = lax.rem(s + i, N_SEQ)
            remote(packed_q.at[h, t], q_all.at[h, s], head_send.at[2 + h], head_recv.at[2 + h], t, d).start()
            return carry

        lax.fori_loop(1, N_SEQ, queries_out, 0)
        keep = pltpu.make_async_copy(packed_q.at[h, s], q_all.at[h, s], own.at[2 + h])
        keep.start()
        kept.append(keep)

    for copy in kept:
        copy.wait()
    for copy in (g_mate, mate_down, mate_up, mate_across):
        copy.wait_recv()
    for copy in (g_up, g_down, g_mate, half_up, mate_down, half_down, mate_up, mate_across):
        copy.wait_send()
    for sem in (w_recv.at[1], w_send.at[1]):
        wait_bytes(w_all.at[:, 0 : N_X - 1], sem)
    wait_bytes(came_tag.at[0 : N_DP - 1], slot_send.at[0])
    wait_bytes(came_kv.at[0 : N_DP - 1], slot_send.at[1])
    for h in range(2):
        wait_bytes(came_q.at[h, 0 : N_DP - 1], slot_send.at[2 + h])
    for sems in (head_recv, head_send):
        wait_bytes(k_all.at[0 : N_SEQ - 1], sems.at[0])
        wait_bytes(v_all.at[0 : N_SEQ - 1], sems.at[1])
        for h in range(2):
            wait_bytes(q_all.at[h, 0 : N_SEQ - 1], sems.at[2 + h])


def attention(q_all, k_ref, v_ref, g_all, w_all, doc_ref, dq_all, dk_ref, dv_ref, wo_ref, g_t, o_t, k_t, v_t, doc_c, dk_sum, dv_sum):
    k_t[...] = k_ref[...].astype(F32).T.astype(BF16)
    v_t[...] = v_ref[...].astype(F32).T.astype(BF16)
    doc_row = doc_ref[...].astype(F32)
    doc_c[...] = jnp.broadcast_to(doc_row, (HEAD, SEQ_LEN)).T
    weight = w_all[...].astype(F32).reshape(2 * HEAD, D).astype(BF16)
    for i in range(SEQ_LEN // QB):
        g_t[:, i * QB : (i + 1) * QB] = nt(weight, g_all[i * QB : (i + 1) * QB, :]).astype(BF16)
    dk_sum[...] = jnp.zeros_like(dk_sum)
    dv_sum[...] = jnp.zeros_like(dv_sum)

    def one_head(h, carry):
        rows = pl.ds(pl.multiple_of(h * HEAD, HEAD), HEAD)
        for i in range(SEQ_LEN // QB):
            lo, hi = max(0, i - 2) * QB, (i + 1) * QB
            here = slice(i * QB, hi)
            q_block = q_all[h, here, :]
            keys = doc_c[lo:hi, :]
            same = jnp.concatenate([keys, keys], axis=1) == doc_row[:, here]
            earlier = lax.broadcasted_iota(jnp.int32, (hi - lo, QB), 0) + lo <= lax.broadcasted_iota(
                jnp.int32, (hi - lo, QB), 1
            ) + i * QB
            scores = jnp.where(same & earlier, nt(k_ref[lo:hi, :], q_block) * SOFT_SCALE, NEG_FILL)
            terms = jnp.exp(scores - jnp.max(scores, axis=0, keepdims=True))
            weights = terms * (1.0 / jnp.sum(terms, axis=0, keepdims=True))
            weights_low = weights.astype(BF16)
            out = nn(v_t[:, lo:hi], weights_low).astype(BF16)
            o_t[rows, here] = out
            grad = g_t[rows, here]
            delta = jnp.sum(grad.astype(F32) * out.astype(F32), axis=0, keepdims=True)
            dscores = (weights * (nn(v_ref[lo:hi, :], grad) - delta)).astype(BF16)
            dq_all[h, here, :] = (nn(k_t[:, lo:hi], dscores) * SOFT_SCALE).T.astype(BF16)
            dk_sum[lo:hi, :] += nn(dscores, q_block)
            dv_sum[lo:hi, :] += nt(weights_low, grad)
        return carry

    lax.fori_loop(0, 2, one_head, 0)
    dk_ref[...] = (dk_sum[...] * SOFT_SCALE).astype(BF16)
    dv_ref[...] = dv_sum[...].astype(BF16)
    for c in range(D // 256):
        cols = slice(c * 256, (c + 1) * 256)
        wo_ref[:, :, :, cols] = nn(o_t[...], g_all[:, cols]).reshape(N_Z, N_X, PACK, 256).astype(BF16)


def backward_exchange(
    dq_all, dk_ref, dv_ref, tag_ref, target_ref, wo_ref,
    dq_out, dk_out, dv_out, wo_out,
    came_q, came_k, came_v, slots_q, slots_kv, ret_q, ret_kv, wo_x, wo_mid, wo_z,
    own, head_send, head_recv, slot_send, slot_recv, wo_send, wo_recv,
):
    s, d = lax.axis_index("seq"), lax.axis_index("dp")
    z, x = d // N_X, lax.rem(d, N_X)
    barrier = greet(s, d)
    kept = [
        pltpu.make_async_copy(dq_all.at[0, s], came_q.at[0, s], own.at[0]),
        pltpu.make_async_copy(dq_all.at[1, s], came_q.at[1, s], own.at[1]),
        pltpu.make_async_copy(dk_ref.at[s], came_k.at[s], own.at[2]),
        pltpu.make_async_copy(dv_ref.at[s], came_v.at[s], own.at[3]),
        pltpu.make_async_copy(wo_ref.at[:, x], wo_x.at[x], own.at[4]),
    ]
    for copy in kept:
        copy.start()
    for copy in kept:
        copy.wait()
    place = tag_ref[...].astype(F32).reshape(N_DP * PACK, TOK).astype(BF16)
    gather = (lax.broadcasted_iota(jnp.int32, (TOK, N_DP * PACK), 1) == target_ref[...]).astype(F32).astype(BF16)
    wait_greeted(barrier)

    for j, (src, dst) in enumerate(
        ((dq_all.at[0], came_q.at[0]), (dq_all.at[1], came_q.at[1]), (dk_ref, came_k), (dv_ref, came_v))
    ):

        def to_owner(i, carry):
            t = lax.rem(s + i, N_SEQ)
            remote(src.at[t], dst.at[s], head_send.at[j], head_recv.at[j], t, d).start()
            return carry

        lax.fori_loop(1, N_SEQ, to_owner, 0)

    def wo_along_x(i, carry):
        xx = lax.rem(x + i, N_X)
        remote(wo_ref.at[:, xx], wo_x.at[x], wo_send.at[0], wo_recv.at[0], s, z * N_X + xx).start()
        return carry

    lax.fori_loop(1, N_X, wo_along_x, 0)

    for h in range(2):
        wait_bytes(came_q.at[h, 0 : N_SEQ - 1], head_recv.at[h])
        for g in range(N_SEQ):
            slots_q[h, :, :, g * HEAD : (g + 1) * HEAD] = as_slots(nn(place, came_q[h, g]))
        send_slots(slots_q.at[h], ret_q.at[h], slot_send.at[h], slot_recv.at[h], s, d)
    wait_bytes(came_k.at[0 : N_SEQ - 1], head_recv.at[2])
    wait_bytes(came_v.at[0 : N_SEQ - 1], head_recv.at[3])
    for part, ref in enumerate((came_k, came_v)):
        for c in range(4):
            both = (ref[2 * c].astype(F32) + ref[2 * c + 1].astype(F32)).astype(BF16)
            cols = slice(part * 512 + c * HEAD, part * 512 + (c + 1) * HEAD)
            slots_kv[:, :, cols] = as_slots(nn(place, both))
    send_slots(slots_kv, ret_kv, slot_send.at[2], slot_recv.at[2], s, d)
    kept = [
        pltpu.make_async_copy(slots_q.at[0, d], ret_q.at[0, d], own.at[0]),
        pltpu.make_async_copy(slots_q.at[1, d], ret_q.at[1, d], own.at[1]),
        pltpu.make_async_copy(slots_kv.at[d], ret_kv.at[d], own.at[2]),
    ]
    for copy in kept:
        copy.start()

    wait_bytes(wo_x.at[0 : N_X - 1], wo_recv.at[0])
    for c in range(D // 256):
        cols = slice(c * 256, (c + 1) * 256)
        total = wo_x[0, :, :, cols].astype(F32)
        for j in range(1, N_X):
            total += wo_x[j, :, :, cols].astype(F32)
        wo_mid[:, :, cols] = total.astype(BF16)

    def wo_along_z(i, carry):
        zz = lax.rem(z + i, N_Z)
        remote(wo_mid.at[zz], wo_z.at[z], wo_send.at[1], wo_recv.at[1], s, zz * N_X + x).start()
        return carry

    lax.fori_loop(1, N_Z, wo_along_z, 0)
    keep = pltpu.make_async_copy(wo_mid.at[z], wo_z.at[z], own.at[3])
    keep.start()
    for copy in kept:
        copy.wait()
    keep.wait()

    for h in range(2):
        wait_bytes(ret_q.at[h, 0 : N_DP - 1], slot_recv.at[h])
        for c in range(4):
            two = nn(gather, slot_rows(ret_q.at[h], slice(c * 256, (c + 1) * 256))).astype(BF16)
            for e in range(2):
                at = (2 * c + e) * 256 + h * HEAD
                dq_out[:, at : at + HEAD] = two[:, e * HEAD : (e + 1) * HEAD]
    wait_bytes(ret_kv.at[0 : N_DP - 1], slot_recv.at[2])
    for part, ref in enumerate((dk_out, dv_out)):
        for c in range(2):
            at = part * 512 + c * 256
            ref[:, c * 256 : (c + 1) * 256] = nn(gather, slot_rows(ret_kv, slice(at, at + 256))).astype(BF16)
    wait_bytes(wo_z.at[0 : N_Z - 1], wo_recv.at[1])
    total = wo_z[0].astype(F32)
    for j in range(1, N_Z):
        total += wo_z[j].astype(F32)
    wo_out[...] = total * GRAD_SCALE

    for h in range(2):
        wait_bytes(ret_q.at[h, 0 : N_DP - 1], slot_send.at[h])
    wait_bytes(ret_kv.at[0 : N_DP - 1], slot_send.at[2])
    for h in range(2):
        wait_bytes(came_q.at[h, 0 : N_SEQ - 1], head_send.at[h])
    wait_bytes(came_k.at[0 : N_SEQ - 1], head_send.at[2])
    wait_bytes(came_v.at[0 : N_SEQ - 1], head_send.at[3])
    wait_bytes(wo_x.at[0 : N_X - 1], wo_send.at[0])
    wait_bytes(wo_z.at[0 : N_Z - 1], wo_send.at[1])


def sds(shape, dtype=BF16):
    return jax.ShapeDtypeStruct(shape, dtype)


def dma(n):
    return pltpu.SemaphoreType.DMA((n,))


def body(q_rows, key_rows, value_rows, pack_peer, pack_slot, doc_ids, grad_out, out_weight):
    in_block = lax.broadcasted_iota(jnp.int32, (16, PACK), 1)
    target = pack_peer[:, None] * PACK + in_block
    landing = pack_slot[:, None] * PACK + in_block
    slot = (N_DP, PACK)
    q_all, k_all, v_all, tag, g_all, w_all = pl.pallas_call(
        forward_exchange,
        name="forward_exchange",
        out_shape=(
            sds((2, N_SEQ, TOK, HEAD)), sds((N_SEQ, TOK, HEAD)), sds((N_SEQ, TOK, HEAD)), sds((*slot, TOK)),
            sds((N_SEQ, TOK, D)), sds((N_Z, N_X, PACK, D)),
        ),
        in_specs=[VMEM] * 7,
        out_specs=(VMEM,) * 6,
        scratch_shapes=[
            pltpu.VMEM((*slot, TOK), BF16), pltpu.VMEM((*slot, KV_COLS), BF16), pltpu.VMEM((2, *slot, KV_COLS), BF16),
            pltpu.VMEM((*slot, KV_COLS), BF16), pltpu.VMEM((2, *slot, KV_COLS), BF16),
            pltpu.VMEM((8, TOK, HEAD), BF16), pltpu.VMEM((2, 8, TOK, HEAD), BF16),
            dma(4), dma(4), dma(4), dma(4), dma(4), dma(8), dma(8), dma(2), dma(2),
        ],
        compiler_params=pltpu.CompilerParams(collective_id=0, has_side_effects=True, vmem_limit_bytes=40 << 20),
    )(q_rows, key_rows, value_rows, target.reshape(1, TOK), landing.reshape(TOK, 1), grad_out[0], out_weight)

    dq_all, dk_part, dv_part, wo_part = pl.pallas_call(
        attention,
        name="attention",
        out_shape=(
            sds((2, SEQ_LEN, HEAD)), sds((SEQ_LEN, HEAD)), sds((SEQ_LEN, HEAD)), sds((N_Z, N_X, PACK, D)),
        ),
        in_specs=[VMEM] * 6,
        out_specs=(VMEM,) * 4,
        scratch_shapes=[
            pltpu.VMEM((2 * HEAD, SEQ_LEN), BF16), pltpu.VMEM((2 * HEAD, SEQ_LEN), BF16),
            pltpu.VMEM((HEAD, SEQ_LEN), BF16), pltpu.VMEM((HEAD, SEQ_LEN), BF16),
            pltpu.VMEM((SEQ_LEN, HEAD), F32), pltpu.VMEM((SEQ_LEN, HEAD), F32), pltpu.VMEM((SEQ_LEN, HEAD), F32),
        ],
        compiler_params=pltpu.CompilerParams(vmem_limit_bytes=40 << 20),
    )(
        q_all.reshape(2, SEQ_LEN, HEAD), k_all.reshape(SEQ_LEN, HEAD), v_all.reshape(SEQ_LEN, HEAD),
        g_all.reshape(SEQ_LEN, D), w_all, doc_ids,
    )

    return pl.pallas_call(
        backward_exchange,
        name="backward_exchange",
        out_shape=(sds((TOK, D)), sds((TOK, 512)), sds((TOK, 512)), sds((PACK, D), F32)),
        in_specs=[VMEM] * 6,
        out_specs=(VMEM,) * 4,
        scratch_shapes=[
            pltpu.VMEM((2, N_SEQ, TOK, HEAD), BF16), pltpu.VMEM((N_SEQ, TOK, HEAD), BF16),
            pltpu.VMEM((N_SEQ, TOK, HEAD), BF16), pltpu.VMEM((2, *slot, KV_COLS), BF16),
            pltpu.VMEM((*slot, KV_COLS), BF16), pltpu.VMEM((2, *slot, KV_COLS), BF16), pltpu.VMEM((*slot, KV_COLS), BF16),
            pltpu.VMEM((N_X, N_Z, PACK, D), BF16), pltpu.VMEM((N_Z, PACK, D), BF16), pltpu.VMEM((N_Z, PACK, D), BF16),
            dma(5), dma(4), dma(4), dma(3), dma(3), dma(2), dma(2),
        ],
        compiler_params=pltpu.CompilerParams(collective_id=1, has_side_effects=True, vmem_limit_bytes=40 << 20),
    )(
        dq_all.reshape(2, N_SEQ, TOK, HEAD), dk_part.reshape(N_SEQ, TOK, HEAD), dv_part.reshape(N_SEQ, TOK, HEAD),
        tag, target.reshape(TOK, 1), wo_part,
    )


def solution(mesh):
    return jax.shard_map(
        body,
        mesh=mesh,
        in_specs=(
            P(("seq", "dp"), None),
            P(("seq", "dp"), None),
            P(("seq", "dp"), None),
            P(("seq", "dp")),
            P(("seq", "dp")),
            P("dp", None),
            P("dp", "seq", None),
            P(("seq", "dp"), None),
        ),
        out_specs=(
            P(("seq", "dp"), None),
            P(("seq", "dp"), None),
            P(("seq", "dp"), None),
            P(("seq", "dp"), None),
        ),
        check_vma=False,
    )
```

time: 585 us -> 136 us (0.23); the launches traced: 576 us -> 133 us
  waiting for transfers between devices: 331 us -> 0 us
  Pallas kernels: 0 us -> 123 us
  starting transfers between devices: 79 us -> 0 us
  local copies, waits for them, and re-layouts: 49.7 us -> 8.3 us
  loops' own time: 37.5 us -> 0 us
  blocking collectives: 22.8 us -> 0 us
  matrix products: 20.7 us -> 0 us
  other arithmetic: 19.8 us -> 1.47 us
  between operations: 15.9 us -> 0.7 us
    reduce_scatter x2 -> x0, waiting for transfers between devices: 190 us -> none  [the longest x1 190 us: body(): lax.psum_scatter(seq_part, 'dp', scatter_dimension=0, tiled=True)]
    pallas_call x0 -> x3, Pallas kernels: none -> 123 us  [the longest x1 57.6 us: body(): pl.pallas_call(forward_exchange, name='forward_exchange', out_shape=(sds(...]
    all_to_all x14 -> x0, waiting for transfers between devices: 105 us -> none  [the longest x1 21.2 us: body(): lax.all_to_all(to_sources(back_q), 'dp', split_axis=0, concat_axis=0, til...]
    all_to_all x14 -> x0, starting transfers between devices: 79 us -> none  [the longest x1 10.2 us: body(): lax.all_to_all(slot_tag, 'dp', split_axis=0, concat_axis=0, tiled=True)]
    another operation x9 -> x0, loops' own time: 37.5 us -> none  [the longest x1 6.59 us: body(): lax.scan(backward_block, start_sums, block_ids)]
    all_gather x1 -> x0, waiting for transfers between devices: 34.5 us -> none  [body(): lax.all_gather(out_weight, ('seq', 'dp'), axis=0, tiled=True)]
    all_to_all x1 -> x0, blocking collectives: 22.8 us -> none  [body(): lax.all_to_all(to_sources(dv_tok), 'dp', split_axis=0, concat_axis=0, til...]
    dot_general x16 -> x0, matrix products: 20.7 us -> none  [the longest x1 6.25 us: body(): lax.dot_general(grad_tok, lax.all_gather(out_weight, ('seq', 'dp'), axis=...]
  transfers between devices with their start and end apart: 17 -> 0, of which waited for: 15 -> 0; matrix products, arithmetic and copies ran while one was open for 14% -> 0% of each run, Pallas kernels for 0% -> 0%
where the time goes in v1:
time: 136 us; the launch traced here: 133 us
  Pallas kernels  123 us (90%)
  local copies, waits for them, and re-layouts  8.3 us (6%)
  other arithmetic  1.47 us (1%)
    pallas_call x1, Pallas kernels, body(): pl.pallas_call(forward_exchange, name='forward_exchange', out_shape=(sds(...  57.6 us
    pallas_call x1, Pallas kernels, body(): pl.pallas_call(backward_exchange, name='backward_exchange', out_shape=(sd...  54.4 us
    pallas_call x1, Pallas kernels, body(): pl.pallas_call(attention, name='attention', out_shape=(sds((2, SEQ_LEN, H...  10.9 us
    unnamed x16, local copies, waits for them, and re-layouts  8.06 us

profile of v1, /device:TPU:65, one launch (start us, length us, event | category | flops | bytes accessed | tf_op | source)
XLA Modules:
  0.0 133.3 jit_solution(14928542940382097222)
XLA Ops:
  0.6 0.7 broadcast_multiply_fusion.1
  1.3 0.1 iota_add_fusion.1
  1.4 0.1 add.48.target_ref
  1.5 0.7 broadcast_multiply_fusion
  2.1 0.1 iota_add_fusion
  2.2 0.1 add.53.landing_ref
  2.3 0.0 copy-start
  2.3 1.0 copy-done
  3.3 0.0 copy-start.1
  3.3 1.0 copy-done.1
  4.4 0.0 copy-start.2
  4.4 0.9 copy-done.2
  5.3 0.0 copy-start.3
  5.3 0.9 copy-done.3
  6.2 0.0 copy-start.4
  6.2 0.8 copy-done.4
  6.9 57.6 %forward_exchange.1 = (bf16[2,8,128,128]{3,2,1,0:T(8,128)(2,1)S(1)}, bf16[8,128,128]{2,1,0:T(8,128)(2,1)S(1)}, bf16[8,128,128]{2,1,0:T(8,128)(2,1)S(1)}, bf16[32...) custom-call(bf16[128,2048]{1,0:T(8,128)(2,1)S(1)} %copy-done, ...), custom_call_target="tpu_custom_call" | custom-call | tf_op jit(solution)/shard_map/forward_exchange/pallas_call | solution.py:405
  64.5 0.0 copy-start.5
  64.5 0.7 copy-done.5
  65.2 10.9 %attention.1 = (bf16[2,1024,128]{2,1,0:T(8,128)(2,1)S(1)}, bf16[1024,128]{1,0:T(8,128)(2,1)S(1)}, bf16[1024,128]{1,0:T(8,128)(2,1)S(1)}, bf16[8,4,8,2048]{3,2,1,0:T(8,128)(2,1)S(1)}) custom-call(bf16[2,1024,128]{2,1,0:T(8,128)(2,1)S(1)} %bitcast.11, bf16[1024,128]{1,0:T(8,128)(2,1)S(1)} %bitcast.14, bf16[1024,128]{1,0:T(8,128)(2,1)S(1)} %bitcast.15, ...), custom_call_target="tpu_custom_call" | custom-call | tf_op jit(solution)/shard_map/attention/pallas_call | solution.py:423
  76.1 0.1 add.54.target_ref
  76.2 54.4 %backward_exchange.1 = (bf16[128,2048]{1,0:T(8,128)(2,1)S(1)}, bf16[128,512]{1,0:T(8,128)(2,1)S(1)}, bf16[128,512]{1,0:T(8,128)(2,1)S(1)}, f32[8,2048]{1,0:T(8,128)S(1)}) custom-call(bf16[2,8,128,128]{3,2,1,0:T(8,128)(2,1)S(1)} %bitcast.10, bf16[8,128,128]{2,1,0:T(8,128)(2,1)S(1)} %bitcast.12, bf16[8,128,128]{2,1,0:T(8,128)(2,1)S(1)} %bitcast.13, ...), custom_call_target="tpu_custom_call" | custom-call | tf_op jit(solution)/shard_map/backward_exchange/pallas_call | solution.py:442
  130.6 0.8 copy.20
  131.4 0.7 copy.21
  132.0 0.7 copy.22
  132.7 0.6 copy.23
Async XLA Ops:
  2.3 1.0 copy-start
  3.3 1.0 copy-start.1
  4.4 0.9 copy-start.2
  5.3 0.9 copy-start.3
  6.2 0.8 copy-start.4
  64.5 0.7 copy-start.5

commit v2 on v1

v2 whole, which is shorter than its diff:
```python
import math

import jax
import jax.numpy as jnp
from jax import lax
from jax.experimental import pallas as pl
from jax.experimental.pallas import tpu as pltpu
from jax.sharding import PartitionSpec as P

HEAD = 128
PACK = 8
NEG_FILL = -1e30
MESH = pl.DeviceIdType.MESH
BF16 = jnp.bfloat16
F32 = jnp.float32
N_SEQ, N_Y = 8, 4
N_DP, N_Z, N_X = 32, 8, 4
TOK = 128
SEQ_LEN = 1024
D = 2048
KV_COLS = 1024
QB = 256
SOFT_SCALE = 1.0 / math.sqrt(HEAD)
GRAD_SCALE = 8.0 / math.sqrt(N_DP * SEQ_LEN)
VMEM = pl.BlockSpec(memory_space=pltpu.VMEM)
ANY = pl.BlockSpec(memory_space=pl.ANY)


def nn(a, b):
    return lax.dot_general(a, b, (((1,), (0,)), ((), ())), preferred_element_type=F32)


def nt(a, b):
    return lax.dot_general(a, b, (((1,), (1,)), ((), ())), preferred_element_type=F32)


def remote(src, dst, send, recv, seq, dp):
    return pltpu.make_async_remote_copy(
        src_ref=src, dst_ref=dst, send_sem=send, recv_sem=recv, device_id=(seq, dp), device_id_type=MESH
    )


def greet(s, d):
    barrier = pltpu.get_barrier_semaphore()

    def along_dp(i, carry):
        pl.semaphore_signal(barrier, inc=1, device_id=(s, lax.rem(d + i, N_DP)), device_id_type=MESH)
        return carry

    def along_seq(i, carry):
        pl.semaphore_signal(barrier, inc=1, device_id=(lax.rem(s + i, N_SEQ), d), device_id_type=MESH)
        return carry

    lax.fori_loop(1, N_DP, along_dp, 0)
    lax.fori_loop(1, N_SEQ, along_seq, 0)
    return barrier


def wait_greeted(barrier):
    pl.semaphore_wait(barrier, N_DP - 1 + N_SEQ - 1)


def send_slots(slots, came, send, recv, s, d):
    def one(i, carry):
        p = lax.rem(d + i, N_DP)
        remote(slots.at[p], came.at[d], send, recv, s, p).start()
        return carry

    lax.fori_loop(1, N_DP, one, 0)


def wait_bytes(ref, sem):
    pltpu.make_async_copy(ref, ref, sem).wait()


def slot_rows(ref, columns):
    block = ref[:, :, columns]
    return block.astype(F32).reshape(N_DP * PACK, block.shape[2]).astype(BF16)


def as_slots(rows):
    return rows.reshape(N_DP, PACK, rows.shape[1]).astype(BF16)


def each_other(count, me, send):
    def one(i, carry):
        send(lax.rem(me + i, count))
        return carry

    lax.fori_loop(1, count, one, 0)


def rows_of(values, scalars, width):
    chosen = jnp.zeros_like(values)
    for i in range(TOK // PACK):
        chosen = jnp.where(values == i, scalars[i], chosen)
    return chosen * PACK + width


def kernel(
    q_hbm, k_hbm, v_hbm, peer_hbm, slot_hbm, doc_hbm, grad_hbm, w_hbm,
    dq_out, dk_out, dv_out, wo_out,
    peer, slot, q_in, k_in, v_in, doc_in, g_all, w_all,
    slots_kv, slots_q, came_kv, came_q, packed_kv, packed_q, q_all, k_all, v_all,
    g_t, o_t, k_t, v_t, doc_c, dk_sum, dv_sum, dq_all, dk_part, dv_part,
    back_q, back_k, back_v, out_q, out_kv, ret_q, ret_kv, wo_part, wo_x, wo_mid, wo_z,
    own, slot_send, slot_recv, head_send, head_recv, g_send, g_recv, w_send, w_recv,
    back_send, back_recv, out_send, ret_recv, wo_send, wo_recv,
):
    s, d = lax.axis_index("seq"), lax.axis_index("dp")
    y, core = s // 2, lax.rem(s, 2)
    z, x = d // N_X, lax.rem(d, N_X)
    mate = y * 2 + 1 - core
    up, down = lax.rem(y + 1, N_Y) * 2 + core, lax.rem(y + N_Y - 1, N_Y) * 2 + core
    across = lax.rem(y + 2, N_Y) * 2 + core

    inputs = [
        pltpu.make_async_copy(src, dst, own.at[i])
        for i, (src, dst) in enumerate(
            (
                (peer_hbm, peer), (slot_hbm, slot), (k_hbm, k_in), (v_hbm, v_in), (w_hbm, w_all.at[z, x]),
                (grad_hbm.at[0], g_all.at[s]), (q_hbm, q_in), (doc_hbm, doc_in),
            )
        )
    ]
    for copy in inputs:
        copy.start()
    barrier = greet(s, d)

    inputs[0].wait()
    inputs[1].wait()
    lane = lax.broadcasted_iota(jnp.int32, (1, TOK), 1)
    target = rows_of(lane // PACK, peer, lax.rem(lane, PACK))
    place = (lax.broadcasted_iota(jnp.int32, (N_DP * PACK, TOK), 0) == target).astype(F32).astype(BF16)
    row = lax.broadcasted_iota(jnp.int32, (TOK, TOK), 0)
    landing = rows_of(row // PACK, slot, lax.rem(row, PACK))
    tags = (lax.broadcasted_iota(jnp.int32, (TOK, TOK), 1) == landing).astype(F32).astype(BF16)
    slots_kv[:, :, KV_COLS:] = as_slots(nn(place, tags))
    inputs[2].wait()
    inputs[3].wait()
    for part, ref in enumerate((k_in, v_in)):
        for c in range(2):
            cols = slice(part * 512 + c * 256, part * 512 + (c + 1) * 256)
            slots_kv[:, :, cols] = as_slots(nn(place, ref[:, c * 256 : (c + 1) * 256]))
    inputs[4].wait()
    inputs[5].wait()
    wait_greeted(barrier)

    each_other(N_Z, z, lambda p: remote(w_all.at[z, x], w_all.at[z, x], w_send.at[0], w_recv.at[0], s, p * N_X + x).start())
    g_up = remote(g_all.at[s], g_all.at[s], g_send.at[0], g_recv.at[0], up, d)
    g_down = remote(g_all.at[s], g_all.at[s], g_send.at[1], g_recv.at[1], down, d)
    g_mate = remote(g_all.at[s], g_all.at[s], g_send.at[2], g_recv.at[2], mate, d)
    g_up.start()
    g_down.start()
    g_mate.start()
    send_slots(slots_kv, came_kv, slot_send.at[0], slot_recv.at[0], s, d)

    inputs[6].wait()
    inputs[7].wait()
    for g in range(N_SEQ):
        both = nn(place, q_in[:, g * 256 : (g + 1) * 256])
        slots_q[0, :, :, g * HEAD : (g + 1) * HEAD] = as_slots(both[:, :HEAD])
        slots_q[1, :, :, g * HEAD : (g + 1) * HEAD] = as_slots(both[:, HEAD:])
    for h in range(2):
        send_slots(slots_q.at[h], came_q.at[h], slot_send.at[1 + h], slot_recv.at[1 + h], s, d)
    kept = [
        pltpu.make_async_copy(slots_kv.at[d], came_kv.at[d], own.at[0]),
        pltpu.make_async_copy(slots_q.at[0, d], came_q.at[0, d], own.at[1]),
        pltpu.make_async_copy(slots_q.at[1, d], came_q.at[1, d], own.at[2]),
    ]
    for copy in kept:
        copy.start()

    doc_row = doc_in[...].astype(F32)
    doc_c[...] = jnp.broadcast_to(doc_row, (HEAD, SEQ_LEN)).T
    dk_sum[...] = jnp.zeros_like(dk_sum)
    dv_sum[...] = jnp.zeros_like(dv_sum)
    for copy in kept:
        copy.wait()

    wait_bytes(w_all.at[0 : N_Z - 1, 0], w_recv.at[0])
    wait_bytes(w_all.at[0 : N_Z - 1, 0], w_send.at[0])
    each_other(N_X, x, lambda p: remote(w_all.at[:, x], w_all.at[:, x], w_send.at[1], w_recv.at[1], s, z * N_X + p).start())

    g_up.wait_recv()
    from_down = g_all.at[down]
    half_up = remote(from_down.at[0:64], from_down.at[0:64], g_send.at[3], g_recv.at[3], up, d)
    mate_down = remote(from_down, from_down, g_send.at[4], g_recv.at[4], mate, d)
    half_up.start()
    mate_down.start()
    g_down.wait_recv()
    from_up = g_all.at[up]
    half_down = remote(from_up.at[64:128], from_up.at[64:128], g_send.at[5], g_recv.at[5], down, d)
    mate_up = remote(from_up, from_up, g_send.at[6], g_recv.at[6], mate, d)
    half_down.start()
    mate_up.start()

    wait_bytes(came_kv.at[0 : N_DP - 1], slot_recv.at[0])
    tag_rows = came_kv[:, :, KV_COLS:].astype(F32).reshape(N_DP * PACK, TOK)
    scatter = tag_rows.astype(BF16)
    gather = tag_rows.T.astype(BF16)
    for c in range(4):
        two = nn(gather, slot_rows(came_kv, slice(c * 256, (c + 1) * 256))).astype(BF16)
        packed_kv[2 * c] = two[:, :HEAD]
        packed_kv[2 * c + 1] = two[:, HEAD:]

    def keys_out(t):
        remote(packed_kv.at[t // 2], k_all.at[s], head_send.at[0], head_recv.at[0], t, d).start()
        remote(packed_kv.at[4 + t // 2], v_all.at[s], head_send.at[1], head_recv.at[1], t, d).start()

    each_other(N_SEQ, s, keys_out)
    kept = [
        pltpu.make_async_copy(packed_kv.at[s // 2], k_all.at[s], own.at[0]),
        pltpu.make_async_copy(packed_kv.at[4 + s // 2], v_all.at[s], own.at[1]),
    ]
    for copy in kept:
        copy.start()

    half_up.wait_recv()
    half_down.wait_recv()
    from_across = g_all.at[across]
    mate_across = remote(from_across, from_across, g_send.at[7], g_recv.at[7], mate, d)
    mate_across.start()

    for copy in kept:
        copy.wait()
    wait_bytes(k_all.at[0 : N_SEQ - 1], head_recv.at[0])
    wait_bytes(v_all.at[0 : N_SEQ - 1], head_recv.at[1])
    k_t[...] = k_all[...].reshape(SEQ_LEN, HEAD).astype(F32).T.astype(BF16)
    v_t[...] = v_all[...].reshape(SEQ_LEN, HEAD).astype(F32).T.astype(BF16)
    for copy in (g_mate, mate_down, mate_up, mate_across):
        copy.wait_recv()
    wait_bytes(w_all.at[:, 0 : N_X - 1], w_recv.at[1])
    weight = w_all[...].astype(F32).reshape(2 * HEAD, D).astype(BF16)
    for i in range(SEQ_LEN // QB):
        g_t[:, i * QB : (i + 1) * QB] = nt(weight, g_all[2 * i : 2 * i + 2].reshape(QB, D)).astype(BF16)

    def queries_in(h):
        wait_bytes(came_q.at[h, 0 : N_DP - 1], slot_recv.at[1 + h])
        for c in range(4):
            two = nn(gather, slot_rows(came_q.at[h], slice(c * 256, (c + 1) * 256))).astype(BF16)
            packed_q[h, 2 * c] = two[:, :HEAD]
            packed_q[h, 2 * c + 1] = two[:, HEAD:]
        each_other(
            N_SEQ, s, lambda t: remote(packed_q.at[h, t], q_all.at[h, s], head_send.at[2 + h], head_recv.at[2 + h], t, d).start()
        )
        keep = pltpu.make_async_copy(packed_q.at[h, s], q_all.at[h, s], own.at[2 + h])
        keep.start()
        return keep

    def one_head(h):
        rows = slice(h * HEAD, (h + 1) * HEAD)
        for i in range(SEQ_LEN // QB):
            first, last = 2 * max(0, i - 2), 2 * (i + 1)
            lo, hi = first * TOK, last * TOK
            here = slice(i * QB, hi)
            q_block = q_all[h, 2 * i : 2 * i + 2].reshape(QB, HEAD)
            k_block = k_all[first:last].reshape(hi - lo, HEAD)
            v_block = v_all[first:last].reshape(hi - lo, HEAD)
            keys = doc_c[lo:hi, :]
            same = jnp.concatenate([keys, keys], axis=1) == doc_row[:, here]
            earlier = lax.broadcasted_iota(jnp.int32, (hi - lo, QB), 0) + lo <= lax.broadcasted_iota(
                jnp.int32, (hi - lo, QB), 1
            ) + i * QB
            scores = jnp.where(same & earlier, nt(k_block, q_block) * SOFT_SCALE, NEG_FILL)
            terms = jnp.exp(scores - jnp.max(scores, axis=0, keepdims=True))
            weights = terms * (1.0 / jnp.sum(terms, axis=0, keepdims=True))
            weights_low = weights.astype(BF16)
            out = nn(v_t[:, lo:hi], weights_low).astype(BF16)
            o_t[rows, here] = out
            grad = g_t[rows, here]
            delta = jnp.sum(grad.astype(F32) * out.astype(F32), axis=0, keepdims=True)
            dscores = (weights * (nn(v_block, grad) - delta)).astype(BF16)
            dq_block = (nn(k_t[:, lo:hi], dscores) * SOFT_SCALE).T.astype(BF16)
            dq_all[h, 2 * i] = dq_block[:TOK]
            dq_all[h, 2 * i + 1] = dq_block[TOK:]
            dk_sum[lo:hi, :] += nn(dscores, q_block)
            dv_sum[lo:hi, :] += nt(weights_low, grad)

    def to_owners(src, dst, j):
        each_other(N_SEQ, s, lambda t: remote(src.at[t], dst.at[s], back_send.at[j], back_recv.at[j], t, d).start())
        keep = pltpu.make_async_copy(src.at[s], dst.at[s], own.at[4 + j])
        keep.start()
        return keep

    def arrived(keep, dst, j):
        keep.wait()
        wait_bytes(dst.at[0 : N_SEQ - 1], back_recv.at[j])

    def wo_half(h):
        part = slice(4 * h, 4 * h + 4)
        for c in range(D // 256):
            cols = slice(c * 256, (c + 1) * 256)
            product = nn(o_t[h * HEAD : (h + 1) * HEAD, :], g_all[:, :, cols].reshape(SEQ_LEN, 256))
            wo_part[part, :, :, cols] = product.reshape(4, N_X, PACK, 256).astype(BF16)
        each_other(
            N_X, x, lambda p: remote(wo_part.at[part, p], wo_x.at[x, part], wo_send.at[h], wo_recv.at[h], s, z * N_X + p).start()
        )
        keep = pltpu.make_async_copy(wo_part.at[part, x], wo_x.at[x, part], own.at[h])
        keep.start()
        return keep

    def wo_half_sum(h, keep):
        part = slice(4 * h, 4 * h + 4)
        keep.wait()
        wait_bytes(wo_x.at[0 : N_X - 1, part], wo_recv.at[h])
        for c in range(D // 256):
            cols = slice(c * 256, (c + 1) * 256)
            total = wo_x[0, part, :, cols].astype(F32)
            for j in range(1, N_X):
                total += wo_x[j, part, :, cols].astype(F32)
            wo_mid[part, :, cols] = total.astype(BF16)
        for zz in range(4 * h, 4 * h + 4):

            @pl.when(z != zz)
            def _():
                remote(wo_mid.at[zz], wo_z.at[z], wo_send.at[2], wo_recv.at[2], s, zz * N_X + x).start()

    def queries_back(h, keep):
        arrived(keep, back_q.at[h], h)
        for g in range(N_SEQ):
            out_q[h, :, :, g * HEAD : (g + 1) * HEAD] = as_slots(nn(scatter, back_q[h, g]))
        send_slots(out_q.at[h], ret_q.at[h], out_send.at[h], ret_recv.at[h], s, d)
        keep = pltpu.make_async_copy(out_q.at[h, d], ret_q.at[h, d], own.at[2 + h])
        keep.start()
        return keep

    keep_q0 = queries_in(0)
    keep_q0.wait()
    wait_bytes(q_all.at[0, 0 : N_SEQ - 1], head_recv.at[2])
    one_head(0)
    keep_back0 = to_owners(dq_all.at[0], back_q.at[0], 0)
    keep_q1 = queries_in(1)
    keep_ret0 = queries_back(0, keep_back0)
    keep_wo0 = wo_half(0)
    keep_q1.wait()
    wait_bytes(q_all.at[1, 0 : N_SEQ - 1], head_recv.at[3])
    one_head(1)
    keep_back1 = to_owners(dq_all.at[1], back_q.at[1], 1)
    dk_part[...] = (dk_sum[...] * SOFT_SCALE).astype(BF16).reshape(N_SEQ, TOK, HEAD)
    keep_k = to_owners(dk_part, back_k, 2)
    dv_part[...] = dv_sum[...].astype(BF16).reshape(N_SEQ, TOK, HEAD)
    keep_v = to_owners(dv_part, back_v, 3)
    wo_half_sum(0, keep_wo0)
    keep_wo1 = wo_half(1)
    keep_ret1 = queries_back(1, keep_back1)
    arrived(keep_k, back_k, 2)
    arrived(keep_v, back_v, 3)
    for part, ref in enumerate((back_k, back_v)):
        for c in range(4):
            both = (ref[2 * c].astype(F32) + ref[2 * c + 1].astype(F32)).astype(BF16)
            cols = slice(part * 512 + c * HEAD, part * 512 + (c + 1) * HEAD)
            out_kv[:, :, cols] = as_slots(nn(scatter, both))
    send_slots(out_kv, ret_kv, out_send.at[2], ret_recv.at[2], s, d)
    keep_kv = pltpu.make_async_copy(out_kv.at[d], ret_kv.at[d], own.at[4])
    keep_kv.start()
    wo_half_sum(1, keep_wo1)
    keep_mid = pltpu.make_async_copy(wo_mid.at[z], wo_z.at[z], own.at[5])
    keep_mid.start()

    column = lax.broadcasted_iota(jnp.int32, (TOK, N_DP * PACK), 0)
    target = rows_of(column // PACK, peer, lax.rem(column, PACK))
    pick = (lax.broadcasted_iota(jnp.int32, (TOK, N_DP * PACK), 1) == target).astype(F32).astype(BF16)
    for h, keep in enumerate((keep_ret0, keep_ret1)):
        keep.wait()
        wait_bytes(ret_q.at[h, 0 : N_DP - 1], ret_recv.at[h])
        for c in range(4):
            two = nn(pick, slot_rows(ret_q.at[h], slice(c * 256, (c + 1) * 256))).astype(BF16)
            for e in range(2):
                at = (2 * c + e) * 256 + h * HEAD
                dq_out[:, at : at + HEAD] = two[:, e * HEAD : (e + 1) * HEAD]
    keep_kv.wait()
    wait_bytes(ret_kv.at[0 : N_DP - 1], ret_recv.at[2])
    for part, ref in enumerate((dk_out, dv_out)):
        for c in range(2):
            at = part * 512 + c * 256
            ref[:, c * 256 : (c + 1) * 256] = nn(pick, slot_rows(ret_kv, slice(at, at + 256))).astype(BF16)
    keep_mid.wait()
    wait_bytes(wo_z.at[0 : N_Z - 1], wo_recv.at[2])
    total = wo_z[0].astype(F32)
    for j in range(1, N_Z):
        total += wo_z[j].astype(F32)
    wo_out[...] = total * GRAD_SCALE

    for copy in (g_up, g_down, g_mate, half_up, mate_down, half_down, mate_up, mate_across):
        copy.wait_send()
    wait_bytes(w_all.at[:, 0 : N_X - 1], w_send.at[1])
    wait_bytes(came_kv.at[0 : N_DP - 1], slot_send.at[0])
    wait_bytes(k_all.at[0 : N_SEQ - 1], head_send.at[0])
    wait_bytes(v_all.at[0 : N_SEQ - 1], head_send.at[1])
    wait_bytes(back_k.at[0 : N_SEQ - 1], back_send.at[2])
    wait_bytes(back_v.at[0 : N_SEQ - 1], back_send.at[3])
    wait_bytes(ret_kv.at[0 : N_DP - 1], out_send.at[2])
    wait_bytes(wo_z.at[0 : N_Z - 1], wo_send.at[2])
    for h in range(2):
        wait_bytes(came_q.at[h, 0 : N_DP - 1], slot_send.at[1 + h])
        wait_bytes(q_all.at[h, 0 : N_SEQ - 1], head_send.at[2 + h])
        wait_bytes(back_q.at[h, 0 : N_SEQ - 1], back_send.at[h])
        wait_bytes(ret_q.at[h, 0 : N_DP - 1], out_send.at[h])
        wait_bytes(wo_x.at[0 : N_X - 1, 4 * h : 4 * h + 4], wo_send.at[h])


def body(q_rows, key_rows, value_rows, pack_peer, pack_slot, doc_ids, grad_out, out_weight):
    def sds(shape, dtype=BF16):
        return jax.ShapeDtypeStruct(shape, dtype)

    def buf(*shape, dtype=BF16):
        return pltpu.VMEM(shape, dtype)

    slot = (N_DP, PACK)
    heads = (N_SEQ, TOK, HEAD)
    return pl.pallas_call(
        kernel,
        name="attention_backward",
        out_shape=(sds((TOK, D)), sds((TOK, 512)), sds((TOK, 512)), sds((PACK, D), F32)),
        in_specs=[ANY] * 8,
        out_specs=(VMEM,) * 4,
        scratch_shapes=[
            pltpu.SMEM((16,), jnp.int32), pltpu.SMEM((16,), jnp.int32),
            buf(TOK, D), buf(TOK, 512), buf(TOK, 512), buf(1, SEQ_LEN, dtype=jnp.int32),
            buf(N_SEQ, TOK, D), buf(N_Z, N_X, PACK, D),
            buf(*slot, KV_COLS + TOK), buf(2, *slot, KV_COLS), buf(*slot, KV_COLS + TOK), buf(2, *slot, KV_COLS),
            buf(*heads), buf(2, *heads), buf(2, *heads), buf(*heads), buf(*heads),
            buf(2 * HEAD, SEQ_LEN), buf(2 * HEAD, SEQ_LEN), buf(HEAD, SEQ_LEN), buf(HEAD, SEQ_LEN),
            buf(SEQ_LEN, HEAD, dtype=F32), buf(SEQ_LEN, HEAD, dtype=F32), buf(SEQ_LEN, HEAD, dtype=F32),
            buf(2, *heads), buf(*heads), buf(*heads),
            buf(2, *heads), buf(*heads), buf(*heads),
            buf(2, *slot, KV_COLS), buf(*slot, KV_COLS), buf(2, *slot, KV_COLS), buf(*slot, KV_COLS),
            buf(N_Z, N_X, PACK, D), buf(N_X, N_Z, PACK, D), buf(N_Z, PACK, D), buf(N_Z, PACK, D),
            *(pltpu.SemaphoreType.DMA((n,)) for n in (8, 3, 3, 4, 4, 8, 8, 2, 2, 4, 4, 3, 3, 3, 3)),
        ],
        compiler_params=pltpu.CompilerParams(collective_id=0, has_side_effects=True, vmem_limit_bytes=60 << 20),
    )(q_rows, key_rows, value_rows, pack_peer, pack_slot, doc_ids, grad_out, out_weight)


def solution(mesh):
    return jax.shard_map(
        body,
        mesh=mesh,
        in_specs=(
            P(("seq", "dp"), None),
            P(("seq", "dp"), None),
            P(("seq", "dp"), None),
            P(("seq", "dp")),
            P(("seq", "dp")),
            P("dp", None),
            P("dp", "seq", None),
            P(("seq", "dp"), None),
        ),
        out_specs=(
            P(("seq", "dp"), None),
            P(("seq", "dp"), None),
            P(("seq", "dp"), None),
            P(("seq", "dp"), None),
        ),
        check_vma=False,
    )
```

time: 136 us -> 112 us (0.82)
  Pallas kernels: 123 us -> 105 us
  local copies, waits for them, and re-layouts: 8.3 us -> 4.36 us
  other arithmetic: 1.47 us -> 0 us
    pallas_call x3 -> x1, Pallas kernels: 123 us -> 105 us  [body(): pl.pallas_call(kernel, name='attention_backward', out_shape=(sds((TOK, D)...]
    unnamed x16 -> x10, local copies, waits for them, and re-layouts: 8.06 us -> 4.36 us
where the time goes in v2:
time: 112 us; the launch traced here: 110 us
  Pallas kernels  105 us (94%)
  local copies, waits for them, and re-layouts  4.36 us (4%)
    pallas_call x1, Pallas kernels, body(): pl.pallas_call(kernel, name='attention_backward', out_shape=(sds((TOK, D)...  105 us
    unnamed x10, local copies, waits for them, and re-layouts  4.36 us

profile of v2, /device:TPU:65, one launch (start us, length us, event | category | flops | bytes accessed | tf_op | source)
XLA Modules:
  0.0 110.5 jit_solution(13686620971011188314)
XLA Ops:
  0.6 105.5 %attention_backward.1 = (bf16[128,2048]{1,0:T(8,128)(2,1)}, bf16[128,512]{1,0:T(8,128)(2,1)}, bf16[128,512]{1,0:T(8,128)(2,1)}, f32[8,2048]{1,0:T(8,128)}) custom-call(bf16[128,2048]{1,0:T(8,128)(2,1)} %q_hbm.1, bf16[128,512]{1,0:T(8,128)(2,1)} %k_hbm.1, bf16[128,512]{1,0:T(8,128)(2,1)} %v_hbm.1, s32[16]{0:T(128)} %peer_hbm.1, s32[16]{0:T(128)} %slot_hbm.1, ...), custom_call_target="tpu_custom_call" | custom-call | tf_op jit(solution)/shard_map/attention_backward/pallas_call | solution.py:412
  106.1 0.0 copy-start.1
  106.1 1.9 %copy.16 = bf16[128,2048]{1,0:T(8,128)(2,1)} copy(bf16[128,2048]{1,0:T(8,128)(2,1)} %get-tuple-element.8) | data formatting | bytes 1048576
  108.1 0.0 copy-done.1
  108.1 0.0 copy-start
  108.1 0.7 copy.17
  108.7 0.3 copy-done
  109.0 0.0 copy-start.2
  109.0 0.7 copy.18
  109.7 0.2 copy-done.2
  109.9 0.6 copy.19
Async XLA Ops:
  106.1 1.9 %copy-start.1 = (bf16[128,512]{1,0:T(8,128)(2,1)S(1)}, bf16[128,512]{1,0:T(8,128)(2,1)}, u32[]{:S(2)}) copy-start(bf16[128,512]{1,0:T(8,128)(2,1)} %get-tuple-element.9) | copy-start | bytes 393220
  108.1 1.0 copy-start
  109.0 0.9 copy-start.2

commit v3 on v2

--- a/solution.py
+++ b/solution.py
@@ -127,6 +127,18 @@
         copy.start()
     barrier = greet(s, d)
 
+    inputs[4].wait()
+    inputs[5].wait()
+    wait_greeted(barrier)
+
+    each_other(N_Z, z, lambda p: remote(w_all.at[z, x], w_all.at[z, x], w_send.at[0], w_recv.at[0], s, p * N_X + x).start())
+    g_up = remote(g_all.at[s], g_all.at[s], g_send.at[0], g_recv.at[0], up, d)
+    g_down = remote(g_all.at[s], g_all.at[s], g_send.at[1], g_recv.at[1], down, d)
+    g_mate = remote(g_all.at[s], g_all.at[s], g_send.at[2], g_recv.at[2], mate, d)
+    g_up.start()
+    g_down.start()
+    g_mate.start()
+
     inputs[0].wait()
     inputs[1].wait()
     lane = lax.broadcasted_iota(jnp.int32, (1, TOK), 1)
@@ -142,17 +154,6 @@
         for c in range(2):
             cols = slice(part * 512 + c * 256, part * 512 + (c + 1) * 256)
             slots_kv[:, :, cols] = as_slots(nn(place, ref[:, c * 256 : (c + 1) * 256]))
-    inputs[4].wait()
-    inputs[5].wait()
-    wait_greeted(barrier)
-
-    each_other(N_Z, z, lambda p: remote(w_all.at[z, x], w_all.at[z, x], w_send.at[0], w_recv.at[0], s, p * N_X + x).start())
-    g_up = remote(g_all.at[s], g_all.at[s], g_send.at[0], g_recv.at[0], up, d)
-    g_down = remote(g_all.at[s], g_all.at[s], g_send.at[1], g_recv.at[1], down, d)
-    g_mate = remote(g_all.at[s], g_all.at[s], g_send.at[2], g_recv.at[2], mate, d)
-    g_up.start()
-    g_down.start()
-    g_mate.start()
     send_slots(slots_kv, came_kv, slot_send.at[0], slot_recv.at[0], s, d)
 
     inputs[6].wait()
@@ -250,7 +251,7 @@
 
     def one_head(h):
         rows = slice(h * HEAD, (h + 1) * HEAD)
-        for i in range(SEQ_LEN // QB):
+        for i in reversed(range(SEQ_LEN // QB)):
             first, last = 2 * max(0, i - 2), 2 * (i + 1)
             lo, hi = first * TOK, last * TOK
             here = slice(i * QB, hi)
@@ -276,9 +277,21 @@
             dq_all[h, 2 * i + 1] = dq_block[TOK:]
             dk_sum[lo:hi, :] += nn(dscores, q_block)
             dv_sum[lo:hi, :] += nt(weights_low, grad)
-
-    def to_owners(src, dst, j):
-        each_other(N_SEQ, s, lambda t: remote(src.at[t], dst.at[s], back_send.at[j], back_recv.at[j], t, d).start())
+            to_owners(i, dq_all.at[h], back_q.at[h], h)
+            if h == 1:
+                dk_part[2 * i : 2 * i + 2] = (dk_sum[here, :] * SOFT_SCALE).astype(BF16).reshape(2, TOK, HEAD)
+                dv_part[2 * i : 2 * i + 2] = dv_sum[here, :].astype(BF16).reshape(2, TOK, HEAD)
+                to_owners(i, dk_part, back_k, 2)
+                to_owners(i, dv_part, back_v, 3)
+
+    def to_owners(i, src, dst, j):
+        for t in (2 * i, 2 * i + 1):
+
+            @pl.when(s != t)
+            def _():
+                remote(src.at[t], dst.at[s], back_send.at[j], back_recv.at[j], t, d).start()
+
+    def keep_own(src, dst, j):
         keep = pltpu.make_async_copy(src.at[s], dst.at[s], own.at[4 + j])
         keep.start()
         return keep
@@ -329,18 +342,16 @@
     keep_q0.wait()
     wait_bytes(q_all.at[0, 0 : N_SEQ - 1], head_recv.at[2])
     one_head(0)
-    keep_back0 = to_owners(dq_all.at[0], back_q.at[0], 0)
+    keep_back0 = keep_own(dq_all.at[0], back_q.at[0], 0)
+    keep_wo0 = wo_half(0)
     keep_q1 = queries_in(1)
     keep_ret0 = queries_back(0, keep_back0)
-    keep_wo0 = wo_half(0)
     keep_q1.wait()
     wait_bytes(q_all.at[1, 0 : N_SEQ - 1], head_recv.at[3])
     one_head(1)
-    keep_back1 = to_owners(dq_all.at[1], back_q.at[1], 1)
-    dk_part[...] = (dk_sum[...] * SOFT_SCALE).astype(BF16).reshape(N_SEQ, TOK, HEAD)
-    keep_k = to_owners(dk_part, back_k, 2)
-    dv_part[...] = dv_sum[...].astype(BF16).reshape(N_SEQ, TOK, HEAD)
-    keep_v = to_owners(dv_part, back_v, 3)
+    keep_back1 = keep_own(dq_all.at[1], back_q.at[1], 1)
+    keep_k = keep_own(dk_part, back_k, 2)
+    keep_v = keep_own(dv_part, back_v, 3)
     wo_half_sum(0, keep_wo0)
     keep_wo1 = wo_half(1)
     keep_ret1 = queries_back(1, keep_back1)
@@ -400,6 +411,17 @@
         wait_bytes(wo_x.at[0 : N_X - 1, 4 * h : 4 * h + 4], wo_send.at[h])
 
 
+def write_out(*refs):
+    ins, outs, held, (came, gone) = refs[:4], refs[4:8], refs[8:12], refs[12:]
+    for i in range(4):
+        pltpu.make_async_copy(ins[i], held[i], came.at[i]).start()
+    for i in range(4):
+        pltpu.make_async_copy(ins[i], held[i], came.at[i]).wait()
+        pltpu.make_async_copy(held[i], outs[i], gone.at[i]).start()
+    for i in range(4):
+        pltpu.make_async_copy(held[i], outs[i], gone.at[i]).wait()
+
+
 def body(q_rows, key_rows, value_rows, pack_peer, pack_slot, doc_ids, grad_out, out_weight):
     def sds(shape, dtype=BF16):
         return jax.ShapeDtypeStruct(shape, dtype)
@@ -409,7 +431,7 @@
 
     slot = (N_DP, PACK)
     heads = (N_SEQ, TOK, HEAD)
-    return pl.pallas_call(
+    made = pl.pallas_call(
         kernel,
         name="attention_backward",
         out_shape=(sds((TOK, D)), sds((TOK, 512)), sds((TOK, 512)), sds((PACK, D), F32)),
@@ -431,6 +453,17 @@
         ],
         compiler_params=pltpu.CompilerParams(collective_id=0, has_side_effects=True, vmem_limit_bytes=60 << 20),
     )(q_rows, key_rows, value_rows, pack_peer, pack_slot, doc_ids, grad_out, out_weight)
+    return pl.pallas_call(
+        write_out,
+        name="write_out",
+        out_shape=tuple(sds(a.shape, a.dtype) for a in made),
+        in_specs=[ANY] * 4,
+        out_specs=(ANY,) * 4,
+        scratch_shapes=[
+            buf(TOK, D), buf(TOK, 512), buf(TOK, 512), buf(PACK, D, dtype=F32),
+            pltpu.SemaphoreType.DMA((4,)), pltpu.SemaphoreType.DMA((4,)),
+        ],
+    )(*made)
 
 
 def solution(mesh):

time: 112 us -> 107 us (0.955); the launches traced: 110 us -> 107 us
  local copies, waits for them, and re-layouts: 4.36 us -> 0 us
    unnamed x10 -> x0, local copies, waits for them, and re-layouts: 4.36 us -> none
    pallas_call x0 -> x1, Pallas kernels: none -> 2 us  [body(): pl.pallas_call(write_out, name='write_out', out_shape=tuple((sds(a.shape,...]
    pallas_call x1, Pallas kernels: 105 us -> 104 us  [body(): pl.pallas_call(kernel, name='attention_backward', out_shape=(sds((TOK, D)...]
where the time goes in v3:
time: 107 us
  Pallas kernels  106 us (99%)
    pallas_call x1, Pallas kernels, body(): pl.pallas_call(kernel, name='attention_backward', out_shape=(sds((TOK, D)...  104 us

profile of v3, /device:TPU:65, one launch (start us, length us, event | category | flops | bytes accessed | tf_op | source)
XLA Modules:
  0.0 106.8 jit_solution(8434724361880088097)
XLA Ops:
  0.6 104.2 %attention_backward.1 = (bf16[128,2048]{1,0:T(8,128)(2,1)}, bf16[128,512]{1,0:T(8,128)(2,1)}, bf16[128,512]{1,0:T(8,128)(2,1)}, f32[8,2048]{1,0:T(8,128)}) custom-call(bf16[128,2048]{1,0:T(8,128)(2,1)} %q_hbm.1, bf16[128,512]{1,0:T(8,128)(2,1)} %k_hbm.1, bf16[128,512]{1,0:T(8,128)(2,1)} %v_hbm.1, s32[16]{0:T(128)} %peer_hbm.1, s32[16]{0:T(128)} %slot_hbm.1, ...), custom_call_target="tpu_custom_call" | custom-call | tf_op jit(solution)/shard_map/attention_backward/pallas_call | solution.py:434
  104.8 2.0 %write_out.1 = (bf16[128,2048]{1,0:T(8,128)(2,1)}, bf16[128,512]{1,0:T(8,128)(2,1)}, bf16[128,512]{1,0:T(8,128)(2,1)}, f32[8,2048]{1,0:T(8,128)}) custom-call(bf16[128,2048]{1,0:T(8,128)(2,1)} %get-tuple-element.8.refs_0_, bf16[128,512]{1,0:T(8,128)(2,1)} %get-tuple-element.9.refs_1_, bf16[128,512]{1,0:T(8,128)(2,1)} %get-tuple-element.10.refs_2_, ...), custom_call_target="tpu_custom_call" | custom-call | tf_op jit(solution)/shard_map/write_out/pallas_call | solution.py:456
